TPU v7x, 128 devices: a whole 4x4x4 slice. The times are simulated.
128 devices in a mesh: north: 4 (over z), east: 32 (over x, y, core).
Axes of the slice: x: 4, y: 4, z: 4, core: 2. Of those that a mesh axis runs over, the one named last changes fastest.
Arguments:
- destinations: int32 [32768, 1], P(('north', 'east')), may hold values from 0 to 127; in each aligned block of 256 rows (0 to 255, 256 to 511, ...) at most 4 rows name the same one
- cells: int32 [32768, 128], P(('north', 'east')), may hold values from 0 to 16128
- fractions: float32 [32768, 2, 128], P(('north', 'east')), may hold values from 0 to 1
- weights: float32 [32768, 128], P(('north', 'east')), may hold values from 0.1 to 10
- heights: float32 [32768, 128], P(('north', 'east')), may hold values from -6 to 6
- counts: int32 [128], P(('north', 'east')), may hold values from 1 to 256, 28672 in all
Outputs:
- surface: float32 [512, 4096], P('north', 'east')
- residual: float32 [512, 4096], P('north', 'east')
Inputs may be any that keep to these rules, and one draw needn't show every extreme that they name: `destinations`: among the 256 blocks of one holder no tile is named by more than 4 blocks, and 4 is reached; every tile is named by some block. `cells`: k names cell row k // 127 and column k % (127) of the block's tile, so all four corner nodes of a return lie in that tile. Holder h holds live blocks 0 to counts[h] - 1; the largest count is 256.
All inputs are finite; a program needn't handle non-finite values.
Results may differ from a plain program's by a relative error of at most 0.00028.
Values sent between devices are 32-bit elements; how exact they have to be, the bound alone decides.
No kernel may reach another device: no remote copies, remote signals or barrier semaphores. Data moves between devices by JAX's collectives and lax.ppermute only.
A program may use at most 64 MiB of HBM per device.

v0:
```python
import jax
import jax.numpy as jnp
from jax import lax
from jax.sharding import PartitionSpec as P

TR = 128
TC = 128
BLK_DEV = 256
ITERS = 3


smooth_weight = 1.0
tension = 0.75
group_blocks = 64
exact = lax.Precision.HIGHEST


def extended(shard, sides, width):
    for axis, dim in sides:
        count, length = (lax.axis_size(axis), shard.shape[dim])
        up = [(i, (i + 1) % count) for i in range(count - 1)]
        down = [(j, i) for i, j in up]
        last = lax.slice_in_dim(shard, length - width, length, axis=dim)
        initial = lax.slice_in_dim(shard, 0, width, axis=dim)
        before = lax.ppermute(last, axis, up)
        after = lax.ppermute(initial, axis, down)
        shard = jnp.concatenate([before, shard, after], axis=dim)
    return shard


def laplace(field):
    padded = extended(field, (("north", 0), ("east", 1)), 1)
    return padded[2:, 1:-1] + padded[:-2, 1:-1] + padded[1:-1, 2:] + padded[1:-1, :-2] - 4.0 * field


def regular(field):
    inner = laplace(field)
    return smooth_weight * ((1.0 - tension) * laplace(inner) - tension * inner)


def factors(payload, cell_ids, valid, tile_rows, tile_cols):
    points = cell_ids.shape[0] * cell_ids.shape[1]
    flat_cells = cell_ids.reshape(points)
    down = payload[:, 0, :].reshape(points)
    right_off = payload[:, 1, :].reshape(points)
    mass = (payload[:, 2, :] * valid[:, None]).reshape(points)
    height = payload[:, 3, :].reshape(points)
    row_of = flat_cells // (tile_cols - 1)
    col_of = flat_cells % (tile_cols - 1)
    row_ids = lax.broadcasted_iota(jnp.int32, (tile_rows, points), 0)
    row_w = jnp.where(row_ids == row_of[None, :], 1.0 - down[None, :], 0.0)
    row_w = row_w + jnp.where(row_ids == row_of[None, :] + 1, down[None, :], 0.0)
    col_ids = lax.broadcasted_iota(jnp.int32, (points, tile_cols), 1)
    col_w = jnp.where(col_ids == col_of[:, None], 1.0 - right_off[:, None], 0.0)
    col_w = col_w + jnp.where(col_ids == col_of[:, None] + 1, right_off[:, None], 0.0)
    return (row_w, col_w, mass, height)


def interp(row_w, col_w, field):
    along = lax.dot_general(row_w, field, (((0,), (0,)), ((), ())), precision=exact)
    return jnp.sum(along * col_w, axis=1)


def spread(row_w, col_w, values):
    return jnp.dot(row_w * values[None, :], col_w, precision=exact)


def total_sum(value):
    return lax.psum(value, ("north", "east"))


def body(destinations, cells, fractions, weights, heights, counts):
    tile_rows = TR
    tile_cols = TC
    north_n = lax.axis_size("north")
    east_n = lax.axis_size("east")
    tiles = north_n * east_n
    bound = max(2, 2 * BLK_DEV // tiles)
    capacity = tiles * bound
    blocks = destinations.shape[0]
    live_rows = lax.broadcasted_iota(jnp.int32, (blocks,), 0) < counts[0]
    target = destinations[:, 0]
    hits = (target[:, None] == lax.broadcasted_iota(jnp.int32, (blocks, tiles), 1)) & live_rows[
        :, None
    ]
    hits = hits.astype(jnp.int32)
    rank = jnp.sum((jnp.cumsum(hits, axis=0) - hits) * hits, axis=1)
    slot = jnp.where(live_rows, target * bound + rank, capacity)
    payload = jnp.concatenate([fractions, weights[:, None, :], heights[:, None, :]], axis=1)
    send_payload = (
        jnp.zeros((capacity,) + payload.shape[1:], jnp.float32).at[slot].set(payload, mode="drop")
    )
    send_cells = jnp.zeros((capacity, cells.shape[1]), jnp.int32).at[slot].set(cells, mode="drop")
    send_flags = jnp.zeros((capacity,), jnp.int32).at[slot].set(1, mode="drop")
    got_payload, got_cells, got_flags = (
        lax.all_to_all(send_payload, ("north", "east"), split_axis=0, concat_axis=0, tiled=True),
        lax.all_to_all(send_cells, ("north", "east"), split_axis=0, concat_axis=0, tiled=True),
        lax.all_to_all(send_flags, ("north", "east"), split_axis=0, concat_axis=0, tiled=True),
    )
    span = min(group_blocks, capacity)
    live_count = jnp.sum(got_flags)
    order = jnp.argsort(1 - got_flags, stable=True)
    rounds = (live_count + span - 1) // span
    flags_float = got_flags.astype(jnp.float32)

    def load(step):
        picks = lax.dynamic_slice_in_dim(order, step * span, span)
        return factors(
            got_payload[picks], got_cells[picks], flags_float[picks], tile_rows, tile_cols
        )

    empty = jnp.zeros((tile_rows, tile_cols), jnp.float32)

    def gather_right(step, acc):
        row_w, col_w, mass, height = load(step)
        return acc + spread(row_w, col_w, mass * height)

    right = lax.fori_loop(0, rounds, gather_right, empty)

    def points(field):

        def apply_group(step, acc):
            row_w, col_w, mass, height = load(step)
            return acc + spread(row_w, col_w, mass * interp(row_w, col_w, field))

        return lax.fori_loop(0, rounds, apply_group, empty)

    surface = empty
    residual = right
    direction = right
    norm_now = total_sum(jnp.sum(residual * residual))
    for step in range(ITERS):
        image = points(direction) + regular(direction)
        alpha = norm_now / lax.psum(jnp.sum(direction * image), ("north", "east"))
        surface = surface + alpha * direction
        residual = residual - alpha * image
        norm_next = total_sum(jnp.sum(residual * residual))
        direction = residual + norm_next / norm_now * direction
        norm_now = norm_next
    return (surface, residual)


def solution(mesh):
    return jax.shard_map(
        body,
        mesh=mesh,
        in_specs=(
            P(("north", "east"), None),
            P(("north", "east"), None),
            P(("north", "east"), None, None),
            P(("north", "east"), None),
            P(("north", "east"), None),
            P(("north", "east")),
        ),
        out_specs=(P("north", "east"), P("north", "east")),
        check_vma=False,
    )
```

profile of v0, /device:TPU:1, one launch (start us, length us, event | category | flops | bytes accessed | tf_op | source)
XLA Modules:
  0.0 974.7 jit_solution(14702689658302601873)
XLA Ops:
  6.4 11.5 %all-to-all-start = ((s32[128,4,1]{1,2,0:T(1,128)}), s32[128,4,1]{1,2,0:T(1,128)S(1)}, u32[]{:S(2)}, u32[]{:S(2)}) async-start(s32[128,4,1]{1,2,0:T(1,128)} %bitcast.37), calls=%async_computation | async-start | bytes 131072 | tf_op jit(solution)/shard_map/all_to_all | solution.py:98
  20.1 7.3 all-to-all-done
  27.4 4.4 all-to-all-start.1
  33.3 24.5 %scatter_fusion = f32[512,4,128]{2,1,0:T(4,128)} fusion(f32[512,4,128]{2,1,0:T(4,128)} %broadcast_in_dim.314, s32[256]{0:T(256)S(1)} %bitcast.272, f32[256,4,128]{2,1,0:T(4,128)S(1)} %pad_maximum_fusion), kind=kCustom, calls=%fused_computation.14 | custom fusion | bytes 1573888 | tf_op jit(solution)/shard_map/scatter | solution.py:91
  57.8 9.7 all-to-all-start.2
  73.2 13.2 %all-to-all-done.2 = f32[512,4,128]{2,1,0:T(4,128)S(1)} async-done(((f32[512,4,128]{2,1,0:T(4,128)}), f32[512,4,128]{2,1,0:T(4,128)S(1)}, u32[]{:S(2)}, u32[]{:S(2)}) %all-to-all-start.2) | async-done | bytes 1048608 | tf_op jit(solution)/shard_map/all_to_all | solution.py:96
  86.4 75.3 %while.48 = (s32[]{:T(128)}, f32[128,128]{1,0:T(8,128)S(1)}, s32[]{:T(128)}, s32[512]{0:T(512)S(1)}, s32[512,128]{1,0:T(8,128)S(1)}, /*index=5*/f32[512,4,128]{2...) while((s32[]{:T(128)}, f32[128,128]{1,0:T(8,128)S(1)}, ...), condition=%wide.region_9.10_spmd, body=%wide.region_8.9_spmd.sunk | while | flops 1622312192 | bytes 1415583 | solution.py:118
  88.8 16.4 %fusion.206 = f32[128,128]{1,0:T(8,128)S(1)} fusion(f32[128,128]{1,0:T(8,128)S(1)} %get-tuple-element.842, f32[8192]{0:T(1024)S(1)} %bitcast.257, s32[8192]{0:T(1024)S(1)} %get-tuple-element.770, f32[8192]{0:T(1024)S(1)} %get-tuple-element.773, s32[8192]{0:T(1024)S(1)} %get-tuple-element.774, f32[8192]{0:T(1024)S(1)} %get-tuple-element.775, ...), kind=kOutput, calls=%fused_computation.38.clone.1 | convolution fusion | flops 1622163456 | bytes 425984 | tf_op jit(solution)/shard_map/while/body/dot_general | solution.py:65
  107.6 16.4 %fusion.206 = f32[128,128]{1,0:T(8,128)S(1)} fusion(f32[128,128]{1,0:T(8,128)S(1)} %get-tuple-element.842, f32[8192]{0:T(1024)S(1)} %bitcast.257, s32[8192]{0:T(1024)S(1)} %get-tuple-element.770, f32[8192]{0:T(1024)S(1)} %get-tuple-element.773, s32[8192]{0:T(1024)S(1)} %get-tuple-element.774, f32[8192]{0:T(1024)S(1)} %get-tuple-element.775, ...), kind=kOutput, calls=%fused_computation.38.clone.1 | convolution fusion | flops 1622163456 | bytes 425984 | tf_op jit(solution)/shard_map/while/body/dot_general | solution.py:65
  126.4 16.4 %fusion.206 = f32[128,128]{1,0:T(8,128)S(1)} fusion(f32[128,128]{1,0:T(8,128)S(1)} %get-tuple-element.842, f32[8192]{0:T(1024)S(1)} %bitcast.257, s32[8192]{0:T(1024)S(1)} %get-tuple-element.770, f32[8192]{0:T(1024)S(1)} %get-tuple-element.773, s32[8192]{0:T(1024)S(1)} %get-tuple-element.774, f32[8192]{0:T(1024)S(1)} %get-tuple-element.775, ...), kind=kOutput, calls=%fused_computation.38.clone.1 | convolution fusion | flops 1622163456 | bytes 425984 | tf_op jit(solution)/shard_map/while/body/dot_general | solution.py:65
  145.3 16.4 %fusion.206 = f32[128,128]{1,0:T(8,128)S(1)} fusion(f32[128,128]{1,0:T(8,128)S(1)} %get-tuple-element.842, f32[8192]{0:T(1024)S(1)} %bitcast.257, s32[8192]{0:T(1024)S(1)} %get-tuple-element.770, f32[8192]{0:T(1024)S(1)} %get-tuple-element.773, s32[8192]{0:T(1024)S(1)} %get-tuple-element.774, f32[8192]{0:T(1024)S(1)} %get-tuple-element.775, ...), kind=kOutput, calls=%fused_computation.38.clone.1 | convolution fusion | flops 1622163456 | bytes 425984 | tf_op jit(solution)/shard_map/while/body/dot_general | solution.py:65
  176.8 4.5 collective-permute-start.5
  184.0 5.1 collective-permute-start.7
  189.2 55.9 %while.49 = (s32[]{:T(128)}, f32[128,128]{1,0:T(8,128)S(1)}, s32[]{:T(128)}, s32[512]{0:T(512)S(1)}, s32[512,128]{1,0:T(8,128)S(1)}, /*index=5*/f32[512,4,128]{2...) while((s32[]{:T(128)}, f32[128,128]{1,0:T(8,128)S(1)}, ...), condition=%wide.region_14.15_spmd, body=%wide.region_12.14_spmd.sunk | while | flops 3245499648 | bytes 1710503 | solution.py:126
  190.9 5.9 fusion.210
  197.7 5.6 fusion.212
  204.8 5.9 fusion.210
  211.6 5.6 fusion.212
  218.7 6.0 fusion.210
  225.6 5.6 fusion.212
  232.6 5.9 fusion.210
  239.5 5.6 fusion.212
  245.9 190.5 %all-reduce = (f32[]{:T(128)}, f32[]{:T(128)}) all-reduce(f32[]{:T(128)} %get-tuple-element.425, f32[]{:T(128)} %get-tuple-element.424), channel_id=1, replica_groups=mesh['north'=4,'east'=32] {'north','east'}, use_global_device_ids=true, to_apply=%region_11.12 | all-reduce | flops 2 | bytes 16 | tf_op jit(solution)/shard_map/psum | solution.py:69
  438.3 64.2 %psum.44 = f32[]{:T(128)} all-reduce(f32[]{:T(128)} %multiply_reduce_fusion.3), channel_id=1, replica_groups=mesh['north'=4,'east'=32] {'north','east'}, use_global_device_ids=true, to_apply=%region_18.19 | all-reduce | flops 1 | bytes 8 | tf_op jit(solution)/shard_map/psum | solution.py:69
  509.9 4.4 collective-permute-start.10
  519.0 4.5 collective-permute-start.13
  531.4 55.7 %while.50 = (s32[]{:T(128)}, f32[128,128]{1,0:T(8,128)S(1)}, s32[]{:T(128)}, s32[512]{0:T(512)S(1)}, s32[512,128]{1,0:T(8,128)S(1)}, /*index=5*/f32[512,4,128]{2...) while((s32[]{:T(128)}, f32[128,128]{1,0:T(8,128)S(1)}, ...), condition=%wide.region_21.22_spmd, body=%wide.region_19.21_spmd.sunk | while | flops 3245499648 | bytes 1710503 | solution.py:126
  532.9 5.9 fusion.216
  539.7 5.6 fusion.218
  546.8 5.9 fusion.216
  553.6 5.6 fusion.218
  560.7 6.0 fusion.216
  567.6 5.6 fusion.218
  574.7 5.9 fusion.216
  581.5 5.6 fusion.218
  587.8 116.5 %psum.45 = f32[]{:T(128)} all-reduce(f32[]{:T(128)} %get-tuple-element.496), channel_id=1, replica_groups=mesh['north'=4,'east'=32] {'north','east'}, use_global_device_ids=true, to_apply=%region_23.24 | all-reduce | flops 1 | bytes 8 | tf_op jit(solution)/shard_map/psum | solution.py:134
  706.3 64.4 %psum.46 = f32[]{:T(128)} all-reduce(f32[]{:T(128)} %get-tuple-element.494), channel_id=1, replica_groups=mesh['north'=4,'east'=32] {'north','east'}, use_global_device_ids=true, to_apply=%region_25.26 | all-reduce | flops 1 | bytes 8 | tf_op jit(solution)/shard_map/psum | solution.py:69
  786.9 4.5 collective-permute-start.21
  799.3 55.7 %while.51 = (s32[]{:T(128)}, f32[128,128]{1,0:T(8,128)S(1)}, s32[]{:T(128)}, s32[512]{0:T(512)S(1)}, s32[512,128]{1,0:T(8,128)S(1)}, /*index=5*/f32[512,4,128]{2...) while((s32[]{:T(128)}, f32[128,128]{1,0:T(8,128)S(1)}, ...), condition=%wide.region_28.29_spmd, body=%wide.region_26.28_spmd.sunk | while | flops 3245499648 | bytes 1710503 | solution.py:126
  800.8 6.0 fusion.222
  807.6 5.6 fusion.224
  814.7 6.0 fusion.222
  821.5 5.6 fusion.224
  828.6 6.0 fusion.222
  835.5 5.6 fusion.224
  842.5 5.9 fusion.222
  849.4 5.6 fusion.224
  855.7 116.6 %psum.47 = f32[]{:T(128)} all-reduce(f32[]{:T(128)} %get-tuple-element.492), channel_id=1, replica_groups=mesh['north'=4,'east'=32] {'north','east'}, use_global_device_ids=true, to_apply=%region_30.31 | all-reduce | flops 1 | bytes 8 | tf_op jit(solution)/shard_map/psum | solution.py:134
  (251 shorter events, 114.2 us)
Async XLA Ops:
  0.6 31.2 %copy-start.2 = (f32[256,128]{1,0:T(8,128)S(1)}, f32[256,128]{1,0:T(8,128)}, u32[]{:S(2)}) copy-start(f32[256,128]{1,0:T(8,128)} %param.17) | copy-start | bytes 393220
  0.6 31.2 %copy-start.1 = (f32[256,128]{1,0:T(8,128)S(1)}, f32[256,128]{1,0:T(8,128)}, u32[]{:S(2)}) copy-start(f32[256,128]{1,0:T(8,128)} %param.18) | copy-start | bytes 393220
  0.7 31.2 %copy-start = (f32[256,2,128]{2,1,0:T(2,128)S(1)}, f32[256,2,128]{2,1,0:T(2,128)}, u32[]{:S(2)}) copy-start(f32[256,2,128]{2,1,0:T(2,128)} %param.16) | copy-start | bytes 786436
  6.4 21.0 %all-to-all-start = ((s32[128,4,1]{1,2,0:T(1,128)}), s32[128,4,1]{1,2,0:T(1,128)S(1)}, u32[]{:S(2)}, u32[]{:S(2)}) async-start(s32[128,4,1]{1,2,0:T(1,128)} %bitcast.37), calls=%async_computation | async-start | bytes 131072 | tf_op jit(solution)/shard_map/all_to_all | solution.py:98
  27.4 30.4 %all-to-all-start.1 = ((s32[128,4,128]{2,1,0:T(4,128)}), s32[128,4,128]{2,1,0:T(4,128)S(1)}, u32[]{:S(2)}, u32[]{:S(2)}) async-start(s32[128,4,128]{2,1,0:T(4,128)} %bitcast.38), calls=%async_computation.1 | async-start | bytes 524288 | tf_op jit(solution)/shard_map/all_to_all | solution.py:97
  57.8 28.6 %all-to-all-start.2 = ((f32[512,4,128]{2,1,0:T(4,128)}), f32[512,4,128]{2,1,0:T(4,128)S(1)}, u32[]{:S(2)}, u32[]{:S(2)}) async-start(f32[512,4,128]{2,1,0:T(4,128)} %scatter_fusion), calls=%async_computation.2 | async-start | bytes 2097152 | tf_op jit(solution)/shard_map/all_to_all | solution.py:96
  161.7 5.3 collective-permute-start
  163.0 4.7 collective-permute-start.1
  167.8 6.2 collective-permute-start.2
  170.9 4.4 collective-permute-start.3
  175.5 5.8 collective-permute-start.4
  176.8 5.2 collective-permute-start.5
  182.1 63.0 %collective-permute-start.6 = (f32[130,1]{1,0:T(8,128)S(1)}, f32[130,1]{1,0:T(8,128)S(1)}, u32[]{:S(2)}, u32[]{:S(2)}) collective-permute-start(f32[130,1]{1,0:T(8,128)S(1)} %get-tuple-element.544), channel_id=1, source_target_pairs={{1,0},{2,1},{3,2},{4,3},{5,4},{6,5},{7,6},{8,7},{9,8},{10,9},{11,1... | collective-permute-start | bytes 1568 | tf_op jit(solution)/shard_map/ppermute | solution.py:26
  184.0 61.0 %collective-permute-start.7 = (f32[130,1]{1,0:T(8,128)S(1)}, f32[130,1]{1,0:T(8,128)S(1)}, u32[]{:S(2)}, u32[]{:S(2)}) collective-permute-start(f32[130,1]{1,0:T(8,128)S(1)} %get-tuple-element.545), channel_id=1, source_target_pairs={{0,1},{1,2},{2,3},{3,4},{4,5},{5,6},{6,7},{7,8},{8,9},{9,10},{10,1... | collective-permute-start | bytes 1568 | tf_op jit(solution)/shard_map/ppermute | solution.py:25
  503.8 5.3 collective-permute-start.8
  505.1 4.7 collective-permute-start.9
  509.9 6.3 collective-permute-start.10
  514.3 3.3 collective-permute-start.11
  517.7 5.8 collective-permute-start.12
  519.0 5.2 collective-permute-start.13
  524.3 62.8 %collective-permute-start.14 = (f32[130,1]{1,0:T(8,128)S(1)}, f32[130,1]{1,0:T(8,128)S(1)}, u32[]{:S(2)}, u32[]{:S(2)}) collective-permute-start(f32[130,1]{1,0:T(8,128)S(1)} %get-tuple-element.540), channel_id=1, source_target_pairs={{1,0},{2,1},{3,2},{4,3},{5,4},{6,5},{7,6},{8,7},{9,8},{10,9},{11,1... | collective-permute-start | bytes 1568 | tf_op jit(solution)/shard_map/ppermute | solution.py:26
  527.1 60.0 %collective-permute-start.15 = (f32[130,1]{1,0:T(8,128)S(1)}, f32[130,1]{1,0:T(8,128)S(1)}, u32[]{:S(2)}, u32[]{:S(2)}) collective-permute-start(f32[130,1]{1,0:T(8,128)S(1)} %get-tuple-element.541), channel_id=1, source_target_pairs={{0,1},{1,2},{2,3},{3,4},{4,5},{5,6},{6,7},{7,8},{8,9},{9,10},{10,1... | collective-permute-start | bytes 1568 | tf_op jit(solution)/shard_map/ppermute | solution.py:25
  772.1 5.3 collective-permute-start.16
  773.4 4.7 collective-permute-start.17
  778.1 5.9 collective-permute-start.18
  782.2 3.3 collective-permute-start.19
  785.6 5.8 collective-permute-start.20
  786.9 5.2 collective-permute-start.21
  792.2 62.8 %collective-permute-start.22 = (f32[130,1]{1,0:T(8,128)S(1)}, f32[130,1]{1,0:T(8,128)S(1)}, u32[]{:S(2)}, u32[]{:S(2)}) collective-permute-start(f32[130,1]{1,0:T(8,128)S(1)} %get-tuple-element.536), channel_id=1, source_target_pairs={{1,0},{2,1},{3,2},{4,3},{5,4},{6,5},{7,6},{8,7},{9,8},{10,9},{11,1... | collective-permute-start | bytes 1568 | tf_op jit(solution)/shard_map/ppermute | solution.py:26
  795.0 60.0 %collective-permute-start.23 = (f32[130,1]{1,0:T(8,128)S(1)}, f32[130,1]{1,0:T(8,128)S(1)}, u32[]{:S(2)}, u32[]{:S(2)}) collective-permute-start(f32[130,1]{1,0:T(8,128)S(1)} %get-tuple-element.537), channel_id=1, source_target_pairs={{0,1},{1,2},{2,3},{3,4},{4,5},{5,6},{6,7},{7,8},{8,9},{9,10},{10,1... | collective-permute-start | bytes 1568 | tf_op jit(solution)/shard_map/ppermute | solution.py:25
where the time goes:
time: 981 us; the launch traced here: 975 us
  blocking collectives  552 us (56%)
  matrix products  204 us (21%)
  starting transfers between devices  98.3 us (10%)
  local copies, waits for them, and re-layouts  65.5 us (7%)
  waiting for transfers between devices  28.7 us (3%)
  other arithmetic  15.2 us (2%)
    psum x3, blocking collectives, total_sum(): return lax.psum(value, ('north', 'east'))  319 us
    psum x2, blocking collectives, body(): alpha = norm_now / lax.psum(jnp.sum(direction * image), ('north', 'east'))  233 us
    dot_general x16, matrix products, spread(): return jnp.dot(row_w * values[None, :], col_w, precision=exact)  133 us
    dot_general x12, matrix products, interp(): lax.dot_general(row_w, field, (((0,), (0,)), ((), ())), precision=exact)  71.4 us
    ppermute x12, starting transfers between devices, extended(): before = lax.ppermute(last, axis, up)  46 us
    ppermute x12, starting transfers between devices, extended(): after = lax.ppermute(initial, axis, down)  26.7 us
    scatter x1, local copies, waits for them, and re-layouts, body(): jnp.zeros((capacity,) + payload.shape[1:], jnp.float32).at[slot]  24.5 us
  transfers between devices with their start and end apart: 27, of which 11 were waited for; matrix products, arithmetic and copies ran while one was open for 20% of the time, Pallas kernels for 0%

commit v1 on v0

v1 whole, which is shorter than its diff:
```python
import jax
import jax.numpy as jnp
from jax import lax
from jax.experimental import pallas as pl
from jax.experimental.pallas import tpu as pltpu
from jax.sharding import PartitionSpec as P

TR = 128
TC = 128
BLK_DEV = 256
MOST = 4
N_NORTH = 4
N_EAST = 32
TILES = N_NORTH * N_EAST
SHRINK = 1.0 / 64.0
TENSION = 0.75
AXES = ("north", "east")
f32 = jnp.float32
bf16 = jnp.bfloat16

SLOTS = 8
CHUNKS = TILES * MOST // SLOTS
SPAN = SLOTS * 128
BANDS = 16
LEFT_ROWS = BANDS * 64 + 16


def whole(space=pltpu.VMEM):
    return pl.BlockSpec(memory_space=space)


def route_kernel(dest_ref, count_ref, cells_ref, frac_ref, weight_ref, height_ref, out_ref, seen_ref):
    out_ref[...] = jnp.zeros_like(out_ref)

    def clear(k, _):
        seen_ref[k] = 0
        return 0

    lax.fori_loop(0, TILES, clear, 0, unroll=8)

    def place(b, _):
        tile = dest_ref[b]
        rank = seen_ref[tile]
        seen_ref[tile] = rank + 1
        row = pl.ds(b, 1)
        to = pl.ds(rank, 1)
        out_ref[tile, 0, to, :] = cells_ref[row, :].astype(f32)
        out_ref[tile, 1, to, :] = frac_ref[b, 0:1, :]
        out_ref[tile, 2, to, :] = frac_ref[b, 1:2, :]
        out_ref[tile, 3, to, :] = weight_ref[row, :]
        out_ref[tile, 4, to, :] = height_ref[row, :]
        return 0

    lax.fori_loop(0, count_ref[0], place, 0)


def high_low(value):
    high = value.astype(bf16).astype(f32)
    return [high, value - high]


def build(chunk, x_ref, vals_ref, left_ref, right_ref):
    def field(f):
        return jnp.concatenate([x_ref[2 * chunk, f], x_ref[2 * chunk + 1, f]], axis=0)

    cell, d, e, mass, height = [field(f) for f in range(5)]
    i = jnp.floor((cell + 0.5) * (1.0 / 127.0))
    j = cell - 127.0 * i
    lower = i >= 64.0
    i_in = jnp.where(lower, i - 64.0, i)
    place = j + jnp.where(lower, 128.0, 0.0)
    a0, a1, b0, b1 = 1.0 - d, d, 1.0 - e, e
    mh = mass * height
    cols = [mass * b0 * b0, mass * b1 * b1, mass * b0 * b1]
    ends = [mh * b0, mh * b1]
    down, up, mid = [], [], []
    for c in cols:
        down += high_low(c * a1 * a1)
        up += high_low(c * a0 * a0)
        mid += high_low(c * a0 * a1)
    for c in ends:
        down += high_low(c * a1)
        up += high_low(c * a0)
    stack = down + up + mid + [i_in, place]
    for k, v in enumerate(stack):
        vals_ref[k * SLOTS:(k + 1) * SLOTS, :] = v
    iota = lax.broadcasted_iota(jnp.int32, (16, 128), 0).astype(f32).astype(bf16)
    zero = jnp.zeros((16, 128), bf16)
    one = jnp.ones((16, 128), bf16)

    def row(k, s):
        return jnp.broadcast_to(vals_ref[k * SLOTS + s:k * SLOTS + s + 1, :], (16, 128))

    n = len(down)
    for s in range(SLOTS):
        lanes = slice(s * 128, (s + 1) * 128)
        i_row = row(26, s)
        i_b = i_row.astype(bf16)
        i_next = (i_row + 1.0).astype(bf16)
        at = [(iota + float(16 * g)) == i_b for g in range(4)]
        after = [(iota + float(16 * g)) == i_next for g in range(4)]
        for k in range(n):
            v1 = row(k, s).astype(bf16)
            v0 = row(n + k, s).astype(bf16)
            for g in range(4):
                left_ref[k * 64 + 16 * g:k * 64 + 16 * g + 16, lanes] = jnp.where(
                    at[g], v0, jnp.where(after[g], v1, zero))
        for k in range(6):
            v = row(2 * n + k, s).astype(bf16)
            base = (n + k) * 64
            for g in range(4):
                left_ref[base + 16 * g:base + 16 * g + 16, lanes] = jnp.where(at[g], v, zero)
        spill = vals_ref[pl.ds(s, 16, stride=SLOTS), :]
        left_ref[1024:1040, lanes] = jnp.where(i_row == 63.0, spill, 0.0).astype(bf16)
        p_b = row(27, s).astype(bf16)
        for g in range(16):
            right_ref[16 * g:16 * g + 16, lanes] = jnp.where((iota + float(16 * g)) == p_b, one, zero)


def shifted(a, by, axis):
    return pltpu.roll(a, by % a.shape[axis], axis)


def gather_kernel(x_ref, fields_ref, top_ref, bottom_ref, west_ref, east_ref,
                  vals_ref, left_ref, right_ref, acc_ref):
    acc_ref[...] = jnp.zeros_like(acc_ref)

    def multiply():
        acc_ref[...] += lax.dot_general(
            left_ref[...], right_ref[...], (((1,), (1,)), ((), ())),
            preferred_element_type=f32)

    def step(c, _):
        build(c, x_ref, vals_ref, left_ref, right_ref)
        multiply()
        return 0

    lax.fori_loop(0, CHUNKS, step, 0)

    row_ids = lax.broadcasted_iota(jnp.int32, (TR, TC), 0)

    def band(k):
        part = acc_ref[k * 64:(k + 1) * 64, :]
        full = jnp.concatenate([part[:, :128], part[:, 128:]], axis=0)
        if k < 10:
            extra = jnp.broadcast_to(acc_ref[1024 + k:1025 + k, 0:128], (TR, TC))
            full = full + jnp.where(row_ids == 64, extra, 0.0)
        return full

    def pair(k):
        return band(k) + band(k + 1)

    diag = pair(0) + shifted(pair(2), 1, 1)
    along_east = pair(4)
    rhs = pair(6) + shifted(pair(8), 1, 1)
    along_south = pair(10) + shifted(pair(12), 1, 1)
    cross = pair(14)
    for k, v in enumerate([rhs, diag, along_east, along_south, cross]):
        fields_ref[k] = v
        top_ref[k] = v[0:8]
        bottom_ref[k] = v[120:128]
        t = v.T
        west_ref[k] = t[0:8]
        east_ref[k] = t[120:128]


def corner_kernel(top_ref, bottom_ref, from_west_ref, from_east_ref, north_ref, south_ref):
    lane = lax.broadcasted_iota(jnp.int32, (8, 128), 1)
    for k in range(5):
        w = from_west_ref[k]
        e = shifted(from_east_ref[k], 64, 1)
        north_ref[k] = top_ref[k]
        south_ref[k] = bottom_ref[k]
        north_ref[5 + k] = jnp.where(lane < 64, w, e)
        south_ref[5 + k] = jnp.where(lane >= 64, w, e)


EXT_R = 144
EXT_C = 256


def krylov_kernel(place_ref, fields_ref, from_west_ref, from_east_ref, from_north_ref, from_south_ref,
                  basis_ref, moments_ref):
    gn = place_ref[0]
    ge = place_ref[1]
    rows = lax.broadcasted_iota(jnp.int32, (EXT_R, EXT_C), 0)
    cols = lax.broadcasted_iota(jnp.int32, (EXT_R, EXT_C), 1)
    grow = gn * TR + jnp.where(rows < 136, rows, rows - EXT_R)
    gcol = ge * TC + jnp.where(cols < 192, cols, cols - EXT_C)
    inside = (grow >= 0) & (grow < N_NORTH * TR) & (gcol >= 0) & (gcol < N_EAST * TC)

    ext = []
    for k in range(5):
        w = from_west_ref[k]
        e = from_east_ref[k]
        n = from_north_ref[5 + k]
        s = from_south_ref[5 + k]
        zeros = jnp.zeros((112, 128), f32)
        side = jnp.concatenate([e, zeros, w], axis=0).T
        n_e = shifted(n, 64, 1)
        s_e = shifted(s, 64, 1)
        south_side = jnp.concatenate([s_e, zeros, s], axis=0).T
        north_side = jnp.concatenate([n_e, zeros, n], axis=0).T
        left = jnp.concatenate([fields_ref[k], from_south_ref[k], from_north_ref[k]], axis=0)
        right = jnp.concatenate([side, south_side[0:8], north_side[120:128]], axis=0)
        full = jnp.concatenate([left, right], axis=1)
        ext.append(jnp.where(inside, full, 0.0))
    v0, diag, along_east, along_south, cross = ext

    def laplace(u, u_l, u_r, u_u, u_d):
        return jnp.where(inside, u_l + u_r + u_u + u_d - 4.0 * u, 0.0)

    def operate(u):
        u_r = shifted(u, -1, 1)
        u_l = shifted(u, 1, 1)
        u_d = shifted(u, -1, 0)
        u_u = shifted(u, 1, 0)
        lu = laplace(u, u_l, u_r, u_u, u_d)
        llu = laplace(lu, shifted(lu, 1, 1), shifted(lu, -1, 1), shifted(lu, 1, 0), shifted(lu, -1, 0))
        u_rd = shifted(u_r, -1, 0)
        out = diag * u + along_east * u_r + along_south * u_d + cross * u_rd
        out = out + shifted(along_east * u + cross * u_d, 1, 1)
        out = out + shifted(along_south * u + cross * u_r + shifted(cross * u, 1, 1), 1, 0)
        return (out + (1.0 - TENSION) * llu - TENSION * lu) * SHRINK

    v = [v0]
    for _ in range(3):
        v.append(operate(v[-1]))
    own = [a[0:TR, 0:TC] for a in v]
    for k in range(4):
        basis_ref[k] = own[k]
    pairs = [(0, 0), (0, 1), (1, 1), (1, 2), (2, 2), (2, 3)]
    lane = lax.broadcasted_iota(jnp.int32, (TILES, 128), 1)
    out = jnp.zeros((TILES, 128), f32)
    for k, (p, q) in enumerate(pairs):
        m = jnp.sum(jnp.sum(own[p] * own[q], axis=0, keepdims=True), axis=1, keepdims=True)
        out = jnp.where(lane == k, m, out)
    moments_ref[...] = out


def finish_kernel(moments_ref, basis_ref, surface_ref, residual_ref):
    total = jnp.sum(moments_ref[...], axis=0, keepdims=True)
    m = [total[:, k:k + 1] for k in range(6)]

    def dot(p, q, shift):
        terms = [p[a] * q[b] * m[a + b + shift] for a in range(len(p)) for b in range(len(q))]
        s = terms[0]
        for t in terms[1:]:
            s = s + t
        return s

    one = jnp.ones_like(m[0])
    res = [one]
    direction = [one]
    surf = []
    rr = m[0]
    for it in range(3):
        alpha = rr / dot(direction, direction, 1)
        surf = [(surf[k] if k < len(surf) else 0.0) + alpha * direction[k] for k in range(len(direction))]
        stepped = [jnp.zeros_like(one)] + [alpha * c for c in direction]
        res = [(res[k] if k < len(res) else 0.0) - stepped[k] for k in range(len(stepped))]
        if it < 2:
            fresh = dot(res, res, 0)
            beta = fresh / rr
            direction = [res[k] + (beta * direction[k] if k < len(direction) else 0.0) for k in range(len(res))]
            rr = fresh
    basis = [basis_ref[k] for k in range(4)]
    out = (surf[0] * SHRINK) * basis[0]
    for k in range(1, 3):
        out = out + (surf[k] * SHRINK) * basis[k]
    surface_ref[...] = out
    out = res[0] * basis[0]
    for k in range(1, 4):
        out = out + res[k] * basis[k]
    residual_ref[...] = out


def body(destinations, cells, fractions, weights, heights, counts):
    params = pltpu.CompilerParams(vmem_limit_bytes=40 * 1024 * 1024)
    send = pl.pallas_call(
        route_kernel,
        out_shape=jax.ShapeDtypeStruct((TILES, 5, MOST, 128), f32),
        in_specs=[whole(pltpu.SMEM), whole(pltpu.SMEM)] + [whole()] * 4,
        out_specs=whole(),
        scratch_shapes=[pltpu.SMEM((TILES,), jnp.int32)],
        compiler_params=params,
    )(destinations.reshape(BLK_DEV), counts, cells, fractions, weights, heights)
    got = lax.all_to_all(send, AXES, split_axis=0, concat_axis=0, tiled=True)
    strip = jax.ShapeDtypeStruct((5, 8, 128), f32)
    fields, top, bottom, west, east = pl.pallas_call(
        gather_kernel,
        out_shape=[jax.ShapeDtypeStruct((5, TR, TC), f32)] + [strip] * 4,
        in_specs=[whole()],
        out_specs=[whole()] * 5,
        scratch_shapes=[
            pltpu.VMEM((28 * SLOTS, 128), f32),
            pltpu.VMEM((LEFT_ROWS, SPAN), bf16),
            pltpu.VMEM((256, SPAN), bf16),
            pltpu.VMEM((LEFT_ROWS, 256), f32),
        ],
        compiler_params=params,
    )(got)
    up_e = [(i, (i + 1) % N_EAST) for i in range(N_EAST)]
    down_e = [(j, i) for i, j in up_e]
    up_n = [(i, (i + 1) % N_NORTH) for i in range(N_NORTH)]
    down_n = [(j, i) for i, j in up_n]
    from_west = lax.ppermute(east, "east", up_e)
    from_east = lax.ppermute(west, "east", down_e)
    message = jax.ShapeDtypeStruct((10, 8, 128), f32)
    to_north, to_south = pl.pallas_call(
        corner_kernel,
        out_shape=[message] * 2,
        in_specs=[whole()] * 4,
        out_specs=[whole()] * 2,
    )(top, bottom, from_west, from_east)
    from_north = lax.ppermute(to_south, "north", up_n)
    from_south = lax.ppermute(to_north, "north", down_n)
    place = jnp.stack([lax.axis_index("north"), lax.axis_index("east")]).astype(jnp.int32)
    basis, moments = pl.pallas_call(
        krylov_kernel,
        out_shape=[jax.ShapeDtypeStruct((4, TR, TC), f32), jax.ShapeDtypeStruct((TILES, 128), f32)],
        in_specs=[whole(pltpu.SMEM)] + [whole()] * 5,
        out_specs=[whole()] * 2,
        compiler_params=params,
    )(place, fields, from_west, from_east, from_north, from_south)
    spread = lax.all_to_all(moments, AXES, split_axis=0, concat_axis=0, tiled=True)
    return pl.pallas_call(
        finish_kernel,
        out_shape=[jax.ShapeDtypeStruct((TR, TC), f32)] * 2,
        in_specs=[whole()] * 2,
        out_specs=[whole()] * 2,
        compiler_params=params,
    )(spread, basis)


def solution(mesh):
    return jax.shard_map(
        body,
        mesh=mesh,
        in_specs=(
            P(AXES, None),
            P(AXES, None),
            P(AXES, None, None),
            P(AXES, None),
            P(AXES, None),
            P(AXES),
        ),
        out_specs=(P("north", "east"), P("north", "east")),
        check_vma=False,
    )
```

time: 981 us -> 136 us (0.14)
  blocking collectives: 552 us -> 53.9 us
  matrix products: 204 us -> 0 us
  starting transfers between devices: 98.3 us -> 4 us
  Pallas kernels: 0 us -> 63.6 us
  local copies, waits for them, and re-layouts: 65.5 us -> 7.62 us
  waiting for transfers between devices: 28.7 us -> 4.73 us
  other arithmetic: 15.2 us -> 0.07 us
    psum x5 -> x0, blocking collectives: 552 us -> none  [the longest x3 319 us: total_sum(): return lax.psum(value, ('north', 'east'))]
    dot_general x28 -> x0, matrix products: 204 us -> none  [the longest x16 133 us: spread(): return jnp.dot(row_w * values[None, :], col_w, precision=exact)]
    ppermute x24 -> x4, starting transfers between devices: 72.7 us -> 4 us  [the longest x1 2.67 us: body(): from_south = lax.ppermute(to_north, 'north', down_n)]
    pallas_call x0 -> x5, Pallas kernels: none -> 63.6 us  [the longest x1 55.8 us: body(): pl.pallas_call(gather_kernel, out_shape=[jax.ShapeDtypeStruct((5, TR, TC)...]
    all_to_all x0 -> x2, blocking collectives: none -> 53.9 us  [the longest x1 32.8 us: body(): got = lax.all_to_all(send, AXES, split_axis=0, concat_axis=0, tiled=True)]
    gather x48 -> x0, local copies, waits for them, and re-layouts: 32.8 us -> none  [the longest x16 12.7 us: load(): flags_float[picks]]
    scatter x3 -> x0, local copies, waits for them, and re-layouts: 28.1 us -> none  [the longest x1 24.5 us: body(): jnp.zeros((capacity,) + payload.shape[1:], jnp.float32).at[slot]]
    all_to_all x3 -> x0, starting transfers between devices: 25.6 us -> none  [the longest x1 11.5 us: body(): lax.all_to_all(send_flags, ('north', 'east'), split_axis=0, concat_axis=0...]
  transfers between devices with their start and end apart: 27 -> 4, of which waited for: 11 -> 3; matrix products, arithmetic and copies ran while one was open for 20% -> 0% of each run, Pallas kernels for 0% -> 0%
where the time goes in v1:
time: 136 us; the launch traced here: 135 us
  Pallas kernels  63.6 us (47%)
  blocking collectives  53.9 us (40%)
  local copies, waits for them, and re-layouts  7.62 us (6%)
  waiting for transfers between devices  4.73 us (3%)
  starting transfers between devices  4 us (3%)
    pallas_call x1, Pallas kernels, body(): pl.pallas_call(gather_kernel, out_shape=[jax.ShapeDtypeStruct((5, TR, TC)...  55.8 us
    all_to_all x1, blocking collectives, body(): got = lax.all_to_all(send, AXES, split_axis=0, concat_axis=0, tiled=True)  32.8 us
    all_to_all x1, blocking collectives, body(): lax.all_to_all(moments, AXES, split_axis=0, concat_axis=0, tiled=True)  21 us
    unnamed x22, local copies, waits for them, and re-layouts  7.62 us
    pallas_call x1, Pallas kernels, body(): pl.pallas_call(route_kernel, out_shape=jax.ShapeDtypeStruct((TILES, 5, MO...  3.16 us
  transfers between devices with their start and end apart: 4, of which 3 were waited for; matrix products, arithmetic and copies ran while one was open for 0% of the time, Pallas kernels for 0%

profile of v1, /device:TPU:1, one launch (start us, length us, event | category | flops | bytes accessed | tf_op | source)
XLA Modules:
  0.0 135.2 jit_solution(14206895472452637429)
XLA Ops:
  1.3 0.0 copy-start
  1.3 0.9 copy-done
  2.2 0.0 copy-start.1
  2.2 0.9 copy-done.1
  3.1 0.0 copy-start.2
  3.1 0.9 copy-done.2
  4.0 0.0 copy-start.3
  4.0 0.9 copy-done.3
  4.9 0.0 copy-start.10
  4.9 0.7 copy-done.10
  5.6 3.2 %shard_map.77 = f32[128,5,4,128]{3,2,1,0:T(4,128)S(1)} custom-call(s32[256]{0:T(256)S(1)} %bitcast.9, s32[1]{0:T(128)S(6)} %copy.9.count_ref, s32[256,128]{1,0:T(8,128)S(1)} %copy-done.1, f32[256,2,128]{2,1,0:T(2,128)S(1)} %copy-done, f32[256,128]{1,0:T(8,128)S(1)} %copy-done.2, f32[256,128]{1,0:T(8,128)S(1)} %copy-done.3), custom_call_target="tpu_custom_call" | custom-call | tf_op jit(solution)/shard_map/pallas_call | solution.py:280
  8.8 32.8 %all_to_all.16.x_ref = f32[128,5,4,128]{3,2,1,0:T(4,128)S(1)} all-to-all(f32[128,5,4,128]{3,2,1,0:T(4,128)S(1)} %shard_map.77), channel_id=1, replica_groups=mesh['north'=4,'east'=32] {'north','east'}, dimensions={0} | all-to-all | bytes 2621440 | tf_op jit(solution)/shard_map/all_to_all | solution.py:288
  41.6 55.8 %shard_map.78 = (f32[5,128,128]{2,1,0:T(8,128)S(1)}, f32[5,8,128]{2,1,0:T(8,128)S(1)}, f32[5,8,128]{2,1,0:T(8,128)S(1)}, f32[5,8,128]{2,1,0:T(8,128)S(1)}, f32[5,8,128]{2,1,0:T(8,128)S(1)}) custom-call(f32[128,5,4,128]{3,2,1,0:T(4,128)S(1)} %all_to_all.16.x_ref), custom_call_target="tpu_custom_call" | custom-call | tf_op jit(solution)/shard_map/pallas_call | solution.py:290
  97.4 0.0 copy-start.8
  97.4 0.6 copy-done.8
  98.1 0.0 copy-start.9
  98.1 0.6 copy-done.9
  98.7 1.3 collective-permute-start
  100.0 0.0 collective-permute-start.1
  100.0 0.9 collective-permute-done.from_west_ref
  100.9 0.0 copy-start.4
  100.9 2.3 %collective-permute-done.1.from_east_ref = f32[5,8,128]{2,1,0:T(8,128)S(1)} collective-permute-done((f32[5,8,128]{2,1,0:T(8,128)S(1)}, f32[5,8,128]{2,1,0:T(8,128)S(1)}, u32[]{:S(2)}, u32[]{:S(2)}) %collective-permute-start.1) | collective-permute-done | bytes 20512 | tf_op jit(solution)/shard_map/ppermute | solution.py:308
  103.2 0.0 copy-start.6
  103.2 0.0 copy-done.4
  103.2 0.6 copy-done.6
  103.8 1.5 %shard_map.79 = (f32[10,8,128]{2,1,0:T(8,128)}, f32[10,8,128]{2,1,0:T(8,128)}) custom-call(f32[5,8,128]{2,1,0:T(8,128)} %copy-done.8, f32[5,8,128]{2,1,0:T(8,128)} %copy-done.9, f32[5,8,128]{2,1,0:T(8,128)} %copy-done.4, f32[5,8,128]{2,1,0:T(8,128)} %copy-done.6), custom_call_target="tpu_custom_call" | custom-call | tf_op jit(solution)/shard_map/pallas_call | solution.py:310
  105.3 0.0 collective-permute-start.2
  105.3 2.7 %collective-permute-start.3 = (f32[10,8,128]{2,1,0:T(8,128)}, f32[10,8,128]{2,1,0:T(8,128)S(1)}, u32[]{:S(2)}, u32[]{:S(2)}) collective-permute-start(f32[10,8,128]{2,1,0:T(8,128)} %get-tuple-element.17), channel_id=1, source_target_pairs={{32,0},{64,32},{96,64},{0,96},{33,1},{65,33},{97,65},{1,97},{34,2}... | collective-permute-start | bytes 122888 | tf_op jit(solution)/shard_map/ppermute | solution.py:317
  108.0 0.1 pad_add_fusion.place_ref
  108.0 1.5 %collective-permute-done.2.from_north_ref = f32[10,8,128]{2,1,0:T(8,128)S(1)} collective-permute-done((f32[10,8,128]{2,1,0:T(8,128)}, f32[10,8,128]{2,1,0:T(8,128)S(1)}, u32[]{:S(2)}, u32[]{:S(2)}) %collective-permute-start.2) | collective-permute-done | bytes 40992 | tf_op jit(solution)/shard_map/ppermute | solution.py:316
  109.6 0.0 collective-permute-done.3.from_south_ref
  109.6 0.0 copy-start.5
  109.6 0.7 copy-done.5
  110.3 0.0 copy-start.7
  110.3 0.7 copy-done.7
  111.0 2.3 %shard_map.80 = (f32[4,128,128]{2,1,0:T(8,128)S(1)}, f32[128,128]{1,0:T(8,128)S(1)}) custom-call(s32[2]{0:T(128)S(1)} %pad_add_fusion.place_ref, f32[5,128,128]{2,1,0:T(8,128)S(1)} %get-tuple-element.11.fields_ref, f32[5,8,128]{2,1,0:T(8,128)S(1)} %copy-done.5, f32[5,8,128]{2,1,0:T(8,128)S(1)} %copy-done.7, ...), custom_call_target="tpu_custom_call" | custom-call | tf_op jit(solution)/shard_map/pallas_call | solution.py:319
  113.3 21.0 %all_to_all.17 = f32[128,1,128]{2,1,0:T(1,128)S(1)} all-to-all(f32[128,1,128]{2,1,0:T(1,128)S(1)} %bitcast.8), channel_id=1, replica_groups=mesh['north'=4,'east'=32] {'north','east'}, dimensions={0} | all-to-all | bytes 131072 | tf_op jit(solution)/shard_map/all_to_all | solution.py:326
  134.4 0.9 shard_map.81
Async XLA Ops:
  1.3 1.0 copy-start
  2.2 0.9 copy-start.1
  3.1 0.9 copy-start.2
  4.0 0.9 copy-start.3
  4.9 0.7 copy-start.10
  97.4 0.6 copy-start.8
  98.1 0.6 copy-start.9
  98.7 2.2 %collective-permute-start = (f32[5,8,128]{2,1,0:T(8,128)S(1)}, f32[5,8,128]{2,1,0:T(8,128)S(1)}, u32[]{:S(2)}, u32[]{:S(2)}) collective-permute-start(f32[5,8,128]{2,1,0:T(8,128)S(1)} %get-tuple-element.12), channel_id=1, source_target_pairs={{0,1},{1,2},{2,3},{3,4},{4,5},{5,6},{6,7},{7,8},{8,9},{9,10},{10,1... | collective-permute-start | bytes 61448 | tf_op jit(solution)/shard_map/ppermute | solution.py:307
  100.0 3.2 %collective-permute-start.1 = (f32[5,8,128]{2,1,0:T(8,128)S(1)}, f32[5,8,128]{2,1,0:T(8,128)S(1)}, u32[]{:S(2)}, u32[]{:S(2)}) collective-permute-start(f32[5,8,128]{2,1,0:T(8,128)S(1)} %get-tuple-element.13), channel_id=1, source_target_pairs={{1,0},{2,1},{3,2},{4,3},{5,4},{6,5},{7,6},{8,7},{9,8},{10,9},{11,1... | collective-permute-start | bytes 61448 | tf_op jit(solution)/shard_map/ppermute | solution.py:308
  100.9 2.3 %copy-start.4 = (f32[5,8,128]{2,1,0:T(8,128)}, f32[5,8,128]{2,1,0:T(8,128)S(1)}, u32[]{:S(2)}) copy-start(f32[5,8,128]{2,1,0:T(8,128)S(1)} %collective-permute-done.from_west_ref) | copy-start | bytes 61444
  103.2 0.6 copy-start.6
  105.3 4.3 %collective-permute-start.2 = (f32[10,8,128]{2,1,0:T(8,128)}, f32[10,8,128]{2,1,0:T(8,128)S(1)}, u32[]{:S(2)}, u32[]{:S(2)}) collective-permute-start(f32[10,8,128]{2,1,0:T(8,128)} %get-tuple-element.16), channel_id=1, source_target_pairs={{0,32},{32,64},{64,96},{96,0},{1,33},{33,65},{65,97},{97,1},{2,34}... | collective-permute-start | bytes 122888 | tf_op jit(solution)/shard_map/ppermute | solution.py:316
  105.3 4.3 %collective-permute-start.3 = (f32[10,8,128]{2,1,0:T(8,128)}, f32[10,8,128]{2,1,0:T(8,128)S(1)}, u32[]{:S(2)}, u32[]{:S(2)}) collective-permute-start(f32[10,8,128]{2,1,0:T(8,128)} %get-tuple-element.17), channel_id=1, source_target_pairs={{32,0},{64,32},{96,64},{0,96},{33,1},{65,33},{97,65},{1,97},{34,2}... | collective-permute-start | bytes 122888 | tf_op jit(solution)/shard_map/ppermute | solution.py:317
  109.6 0.7 copy-start.5
  110.3 0.7 copy-start.7

commit v2 on v1

--- a/solution.py
+++ b/solution.py
@@ -18,18 +18,41 @@
 f32 = jnp.float32
 bf16 = jnp.bfloat16
 
-SLOTS = 8
-CHUNKS = TILES * MOST // SLOTS
-SPAN = SLOTS * 128
+UNITS = 8
+GROUPS = TILES * MOST // 128
+HALF = 32
+WINDOW = 2 * HALF
 BANDS = 16
-LEFT_ROWS = BANDS * 64 + 16
+TWO_HOT = 10
+LEFT_ROWS = BANDS * HALF + 16
+REACH = 192
+STEPS = 128 // UNITS
+JOIN = 4
 
 
 def whole(space=pltpu.VMEM):
     return pl.BlockSpec(memory_space=space)
 
 
-def route_kernel(dest_ref, count_ref, cells_ref, frac_ref, weight_ref, height_ref, out_ref, seen_ref):
+def sort_lanes(keys):
+    lane = lax.broadcasted_iota(jnp.int32, keys.shape, 1)
+    size = 2
+    while size <= 128:
+        gap = size // 2
+        while gap >= 1:
+            low = (lane & gap) == 0
+            other = jnp.where(low, pltpu.roll(keys, 128 - gap, 1), pltpu.roll(keys, gap, 1))
+            take_min = low == ((lane & size) == 0)
+            keys = jnp.where(take_min, jnp.minimum(keys, other), jnp.maximum(keys, other))
+            gap //= 2
+        size *= 2
+    return keys
+
+
+SORT_ROWS = 256
+
+
+def route_kernel(dest_ref, count_ref, cells_ref, frac_ref, weight_ref, height_ref, out_ref, seen_ref, sorted_ref):
     out_ref[...] = jnp.zeros_like(out_ref)
 
     def clear(k, _):
@@ -37,18 +60,26 @@
         return 0
 
     lax.fori_loop(0, TILES, clear, 0, unroll=8)
+
+    def arrange(part, _):
+        rows = pl.ds(part * SORT_ROWS, SORT_ROWS)
+        cell = cells_ref[rows, :].astype(f32)
+        lane = lax.broadcasted_iota(jnp.int32, cell.shape, 1).astype(f32)
+        keys = sort_lanes(jnp.floor((cell + 0.5) * (1.0 / 127.0)) * 128.0 + lane)
+        source = (keys - 128.0 * jnp.floor(keys * (1.0 / 128.0))).astype(jnp.int32)
+        values = [cell, frac_ref[rows, 0, :], frac_ref[rows, 1, :], weight_ref[rows, :], height_ref[rows, :]]
+        for f, v in enumerate(values):
+            sorted_ref[f, rows, :] = jnp.take_along_axis(v, source, axis=1)
+        return 0
+
+    lax.fori_loop(0, BLK_DEV // SORT_ROWS, arrange, 0)
 
     def place(b, _):
         tile = dest_ref[b]
         rank = seen_ref[tile]
         seen_ref[tile] = rank + 1
-        row = pl.ds(b, 1)
-        to = pl.ds(rank, 1)
-        out_ref[tile, 0, to, :] = cells_ref[row, :].astype(f32)
-        out_ref[tile, 1, to, :] = frac_ref[b, 0:1, :]
-        out_ref[tile, 2, to, :] = frac_ref[b, 1:2, :]
-        out_ref[tile, 3, to, :] = weight_ref[row, :]
-        out_ref[tile, 4, to, :] = height_ref[row, :]
+        for f in range(5):
+            out_ref[tile, f, pl.ds(rank, 1), :] = sorted_ref[f, pl.ds(b, 1), :]
         return 0
 
     lax.fori_loop(0, count_ref[0], place, 0)
@@ -59,15 +90,18 @@
     return [high, value - high]
 
 
-def build(chunk, x_ref, vals_ref, left_ref, right_ref):
-    def field(f):
-        return jnp.concatenate([x_ref[2 * chunk, f], x_ref[2 * chunk + 1, f]], axis=0)
-
-    cell, d, e, mass, height = [field(f) for f in range(5)]
-    i = jnp.floor((cell + 0.5) * (1.0 / 127.0))
+def row_of(cell):
+    return jnp.floor((cell + 0.5) * (1.0 / 127.0))
+
+
+def build(rank, base, group, by_rank_ref, vals_ref):
+    lanes_in = slice(group * 128, group * 128 + 128)
+    cell, d, e, mass, height = [by_rank_ref[f, pl.ds(rank, UNITS), lanes_in] for f in range(5)]
+    i = row_of(cell)
     j = cell - 127.0 * i
-    lower = i >= 64.0
-    i_in = jnp.where(lower, i - 64.0, i)
+    inner = i - base.astype(f32)
+    lower = inner >= float(HALF)
+    i_in = jnp.where((inner >= 0.0) & (inner < float(WINDOW)), jnp.where(lower, inner - float(HALF), inner), -100.0)
     place = j + jnp.where(lower, 128.0, 0.0)
     a0, a1, b0, b1 = 1.0 - d, d, 1.0 - e, e
     mh = mass * height
@@ -81,40 +115,38 @@
     for c in ends:
         down += high_low(c * a1)
         up += high_low(c * a0)
-    stack = down + up + mid + [i_in, place]
-    for k, v in enumerate(stack):
-        vals_ref[k * SLOTS:(k + 1) * SLOTS, :] = v
+    for k, v in enumerate(down + up + mid + [i_in, place]):
+        vals_ref[group, k * UNITS:(k + 1) * UNITS, :] = v
     iota = lax.broadcasted_iota(jnp.int32, (16, 128), 0).astype(f32).astype(bf16)
     zero = jnp.zeros((16, 128), bf16)
     one = jnp.ones((16, 128), bf16)
 
     def row(k, s):
-        return jnp.broadcast_to(vals_ref[k * SLOTS + s:k * SLOTS + s + 1, :], (16, 128))
-
-    n = len(down)
-    for s in range(SLOTS):
-        lanes = slice(s * 128, (s + 1) * 128)
+        return jnp.broadcast_to(vals_ref[group, k * UNITS + s:k * UNITS + s + 1, :], (16, 128))
+
+    lefts, rights = [], []
+    for s in range(UNITS):
         i_row = row(26, s)
         i_b = i_row.astype(bf16)
         i_next = (i_row + 1.0).astype(bf16)
-        at = [(iota + float(16 * g)) == i_b for g in range(4)]
-        after = [(iota + float(16 * g)) == i_next for g in range(4)]
-        for k in range(n):
+        at = [(iota + float(16 * g)) == i_b for g in range(HALF // 16)]
+        after = [(iota + float(16 * g)) == i_next for g in range(HALF // 16)]
+        pieces = []
+        for k in range(TWO_HOT):
             v1 = row(k, s).astype(bf16)
-            v0 = row(n + k, s).astype(bf16)
-            for g in range(4):
-                left_ref[k * 64 + 16 * g:k * 64 + 16 * g + 16, lanes] = jnp.where(
-                    at[g], v0, jnp.where(after[g], v1, zero))
-        for k in range(6):
-            v = row(2 * n + k, s).astype(bf16)
-            base = (n + k) * 64
-            for g in range(4):
-                left_ref[base + 16 * g:base + 16 * g + 16, lanes] = jnp.where(at[g], v, zero)
-        spill = vals_ref[pl.ds(s, 16, stride=SLOTS), :]
-        left_ref[1024:1040, lanes] = jnp.where(i_row == 63.0, spill, 0.0).astype(bf16)
+            v0 = row(TWO_HOT + k, s).astype(bf16)
+            for g in range(HALF // 16):
+                pieces.append(jnp.where(at[g], v0, jnp.where(after[g], v1, zero)))
+        for k in range(BANDS - TWO_HOT):
+            v = row(2 * TWO_HOT + k, s).astype(bf16)
+            for g in range(HALF // 16):
+                pieces.append(jnp.where(at[g], v, zero))
+        spill = vals_ref[group, pl.ds(s, 16, stride=UNITS), :]
+        pieces.append(jnp.where(i_row == float(HALF - 1), spill, 0.0).astype(bf16))
+        lefts.append(jnp.concatenate(pieces, axis=0))
         p_b = row(27, s).astype(bf16)
-        for g in range(16):
-            right_ref[16 * g:16 * g + 16, lanes] = jnp.where((iota + float(16 * g)) == p_b, one, zero)
+        rights.append(jnp.concatenate([jnp.where((iota + float(16 * g)) == p_b, one, zero) for g in range(16)], axis=0))
+    return lefts, rights
 
 
 def shifted(a, by, axis):
@@ -122,30 +154,74 @@
 
 
 def gather_kernel(x_ref, fields_ref, top_ref, bottom_ref, west_ref, east_ref,
-                  vals_ref, left_ref, right_ref, acc_ref):
+                  by_rank_ref, bounds_ref, limits_ref, items_ref, vals_ref,
+                  acc_ref, sem):
+    low = []
+    high = []
+    for g in range(GROUPS):
+        lanes = slice(g * 128, g * 128 + 128)
+        for f in range(5):
+            by_rank_ref[f, :, lanes] = x_ref[g * 32:g * 32 + 32, f].reshape(128, 128).T
+        i = row_of(by_rank_ref[0, :, lanes])
+        live = by_rank_ref[3, :, lanes] > 0.0
+        low.append(jnp.where(live, i, 1000.0))
+        high.append(jnp.where(live, i, -1.0))
+    least, most = low[0], high[0]
+    for g in range(1, GROUPS):
+        least = jnp.minimum(least, low[g])
+        most = jnp.maximum(most, high[g])
+    bounds_ref[0:8, :] = jnp.broadcast_to(jnp.min(least.T, axis=0, keepdims=True), (8, 128)).astype(jnp.int32)
+    bounds_ref[8:16, :] = jnp.broadcast_to(jnp.max(most.T, axis=0, keepdims=True), (8, 128)).astype(jnp.int32)
+    copy = pltpu.make_async_copy(bounds_ref, limits_ref, sem)
+    copy.start()
     acc_ref[...] = jnp.zeros_like(acc_ref)
-
-    def multiply():
-        acc_ref[...] += lax.dot_general(
-            left_ref[...], right_ref[...], (((1,), (1,)), ((), ())),
-            preferred_element_type=f32)
-
-    def step(c, _):
-        build(c, x_ref, vals_ref, left_ref, right_ref)
-        multiply()
+    copy.wait()
+
+    count = jnp.int32(0)
+    for q in range(STEPS):
+        first = limits_ref[0, q * UNITS]
+        last = limits_ref[8, q * UNITS + UNITS - 1]
+        base = (first // 8) * 8
+        for w in range(2):
+            items_ref[0, count] = q * UNITS
+            items_ref[1, count] = base + w * WINDOW
+            count = count + (base + w * WINDOW <= last).astype(jnp.int32)
+    for extra in range(2):
+        items_ref[0, count + extra] = 0
+        items_ref[1, count + extra] = 1000
+
+    sub = lax.broadcasted_iota(jnp.int32, (8, 128), 0)
+
+    def step(t, _):
+        rank = pl.multiple_of(items_ref[0, t], UNITS)
+        base = pl.multiple_of(items_ref[1, t], 8)
+        out = None
+        for part in range(GROUPS // JOIN):
+            lefts, rights = [], []
+            for g in range(part * JOIN, part * JOIN + JOIN):
+                more = build(rank, base, g, by_rank_ref, vals_ref)
+                lefts += more[0]
+                rights += more[1]
+            piece = lax.dot_general(
+                jnp.concatenate(lefts, axis=1), jnp.concatenate(rights, axis=1),
+                (((1,), (1,)), ((), ())), preferred_element_type=f32)
+            out = piece if out is None else out + piece
+        for k in range(BANDS):
+            for h in range(2):
+                rows = pl.ds(k * REACH + base + h * HALF, HALF)
+                acc_ref[rows, :] += out[k * HALF:(k + 1) * HALF, h * 128:(h + 1) * 128]
+        for k in range(TWO_HOT):
+            for h in range(2):
+                rows = pl.ds(k * REACH + base + (h + 1) * HALF, 8)
+                line = BANDS * HALF + k
+                acc_ref[rows, :] += jnp.where(sub == 0, out[line:line + 1, h * 128:(h + 1) * 128], 0.0)
+
         return 0
 
-    lax.fori_loop(0, CHUNKS, step, 0)
-
-    row_ids = lax.broadcasted_iota(jnp.int32, (TR, TC), 0)
+    lax.fori_loop(0, count, step, 0)
 
     def band(k):
-        part = acc_ref[k * 64:(k + 1) * 64, :]
-        full = jnp.concatenate([part[:, :128], part[:, 128:]], axis=0)
-        if k < 10:
-            extra = jnp.broadcast_to(acc_ref[1024 + k:1025 + k, 0:128], (TR, TC))
-            full = full + jnp.where(row_ids == 64, extra, 0.0)
-        return full
+        return acc_ref[k * REACH:k * REACH + TR, :]
 
     def pair(k):
         return band(k) + band(k + 1)
@@ -282,7 +358,7 @@
         out_shape=jax.ShapeDtypeStruct((TILES, 5, MOST, 128), f32),
         in_specs=[whole(pltpu.SMEM), whole(pltpu.SMEM)] + [whole()] * 4,
         out_specs=whole(),
-        scratch_shapes=[pltpu.SMEM((TILES,), jnp.int32)],
+        scratch_shapes=[pltpu.SMEM((TILES,), jnp.int32), pltpu.VMEM((5, BLK_DEV, 128), f32)],
         compiler_params=params,
     )(destinations.reshape(BLK_DEV), counts, cells, fractions, weights, heights)
     got = lax.all_to_all(send, AXES, split_axis=0, concat_axis=0, tiled=True)
@@ -293,10 +369,13 @@
         in_specs=[whole()],
         out_specs=[whole()] * 5,
         scratch_shapes=[
-            pltpu.VMEM((28 * SLOTS, 128), f32),
-            pltpu.VMEM((LEFT_ROWS, SPAN), bf16),
-            pltpu.VMEM((256, SPAN), bf16),
-            pltpu.VMEM((LEFT_ROWS, 256), f32),
+            pltpu.VMEM((5, 128, GROUPS * 128), f32),
+            pltpu.VMEM((16, 128), jnp.int32),
+            pltpu.SMEM((16, 128), jnp.int32),
+            pltpu.SMEM((2, 2 * STEPS + 8), jnp.int32),
+            pltpu.VMEM((GROUPS, 28 * UNITS, 128), f32),
+            pltpu.VMEM((BANDS * REACH, 128), f32),
+            pltpu.SemaphoreType.DMA,
         ],
         compiler_params=params,
     )(got)
@@ -312,6 +391,7 @@
         out_shape=[message] * 2,
         in_specs=[whole()] * 4,
         out_specs=[whole()] * 2,
+        compiler_params=params,
     )(top, bottom, from_west, from_east)
     from_north = lax.ppermute(to_south, "north", up_n)
     from_south = lax.ppermute(to_north, "north", down_n)

time: 136 us -> 101 us (0.74)
  Pallas kernels: 63.6 us -> 33.1 us
  local copies, waits for them, and re-layouts: 7.62 us -> 4.33 us
    pallas_call x1, Pallas kernels: 55.8 us -> 23.3 us  [body(): pl.pallas_call(gather_kernel, out_shape=[jax.ShapeDtypeStruct((5, TR, TC)...]
    pallas_call x1, Pallas kernels: 3.16 us -> 6.51 us  [body(): pl.pallas_call(route_kernel, out_shape=jax.ShapeDtypeStruct((TILES, 5, MO...]
    unnamed x22 -> x10, local copies, waits for them, and re-layouts: 7.62 us -> 4.33 us
    pallas_call x1, Pallas kernels: 1.48 us -> 0.08 us  [body(): pl.pallas_call(corner_kernel, out_shape=[message] * 2, in_specs=[whole()]...]
where the time goes in v2:
time: 101 us
  blocking collectives  53.7 us (53%)
  Pallas kernels  33.1 us (33%)
  waiting for transfers between devices  4.46 us (4%)
  local copies, waits for them, and re-layouts  4.33 us (4%)
  starting transfers between devices  4.12 us (4%)
  between operations  1.32 us (1%)
    all_to_all x1, blocking collectives, body(): got = lax.all_to_all(send, AXES, split_axis=0, concat_axis=0, tiled=True)  32.7 us
    pallas_call x1, Pallas kernels, body(): pl.pallas_call(gather_kernel, out_shape=[jax.ShapeDtypeStruct((5, TR, TC)...  23.3 us
    all_to_all x1, blocking collectives, body(): lax.all_to_all(moments, AXES, split_axis=0, concat_axis=0, tiled=True)  21 us
    pallas_call x1, Pallas kernels, body(): pl.pallas_call(route_kernel, out_shape=jax.ShapeDtypeStruct((TILES, 5, MO...  6.51 us
    unnamed x10, local copies, waits for them, and re-layouts  4.33 us
    ppermute x1, starting transfers between devices, body(): from_south = lax.ppermute(to_north, 'north', down_n)  2.66 us
    pallas_call x1, Pallas kernels, body(): pl.pallas_call(krylov_kernel, out_shape=[jax.ShapeDtypeStruct((4, TR, TC)...  2.32 us
    ppermute x1, waiting for transfers between devices, body(): from_east = lax.ppermute(west, 'east', down_e)  2.3 us
  transfers between devices with their start and end apart: 4, of which 3 were waited for; matrix products, arithmetic and copies ran while one was open for 0% of the time, Pallas kernels for 0%

profile of v2, /device:TPU:1, one launch (start us, length us, event | category | flops | bytes accessed | tf_op | source)
XLA Modules:
  0.0 101.1 jit_solution(11219084184558567965)
XLA Ops:
  1.3 0.0 copy-start
  1.3 0.9 copy-done
  2.2 0.0 copy-start.1
  2.2 0.9 copy-done.1
  3.1 0.0 copy-start.2
  3.1 0.9 copy-done.2
  4.0 0.0 copy-start.3
  4.0 0.9 copy-done.3
  4.9 0.0 copy-start.4
  4.9 0.7 copy-done.4
  5.6 6.5 %shard_map.77 = f32[128,5,4,128]{3,2,1,0:T(4,128)S(1)} custom-call(s32[256]{0:T(256)S(1)} %bitcast.9, s32[1]{0:T(128)S(6)} %copy.9.count_ref, s32[256,128]{1,0:T(8,128)S(1)} %copy-done.1, f32[256,2,128]{2,1,0:T(2,128)S(1)} %copy-done, f32[256,128]{1,0:T(8,128)S(1)} %copy-done.2, f32[256,128]{1,0:T(8,128)S(1)} %copy-done.3), custom_call_target="tpu_custom_call" | custom-call | tf_op jit(solution)/shard_map/pallas_call | solution.py:356
  12.1 32.7 %all_to_all.16.x_ref = f32[128,5,4,128]{3,2,1,0:T(4,128)S(1)} all-to-all(f32[128,5,4,128]{3,2,1,0:T(4,128)S(1)} %shard_map.77), channel_id=1, replica_groups=mesh['north'=4,'east'=32] {'north','east'}, dimensions={0} | all-to-all | bytes 2621440 | tf_op jit(solution)/shard_map/all_to_all | solution.py:364
  44.8 23.3 %shard_map.78 = (f32[5,128,128]{2,1,0:T(8,128)S(1)}, f32[5,8,128]{2,1,0:T(8,128)S(1)}, f32[5,8,128]{2,1,0:T(8,128)S(1)}, f32[5,8,128]{2,1,0:T(8,128)S(1)}, f32[5,8,128]{2,1,0:T(8,128)S(1)}) custom-call(f32[128,5,4,128]{3,2,1,0:T(4,128)S(1)} %all_to_all.16.x_ref), custom_call_target="tpu_custom_call" | custom-call | tf_op jit(solution)/shard_map/pallas_call | solution.py:366
  68.1 1.4 %collective-permute-start = (f32[5,8,128]{2,1,0:T(8,128)S(1)}, f32[5,8,128]{2,1,0:T(8,128)S(1)}, u32[]{:S(2)}, u32[]{:S(2)}) collective-permute-start(f32[5,8,128]{2,1,0:T(8,128)S(1)} %get-tuple-element.12), channel_id=1, source_target_pairs={{0,1},{1,2},{2,3},{3,4},{4,5},{5,6},{6,7},{7,8},{8,9},{9,10},{10,1... | collective-permute-start | bytes 61448 | tf_op jit(solution)/shard_map/ppermute | solution.py:386
  69.5 0.1 collective-permute-start.1
  69.6 0.8 collective-permute-done.from_west_ref
  70.4 2.3 %collective-permute-done.1.from_east_ref = f32[5,8,128]{2,1,0:T(8,128)S(1)} collective-permute-done((f32[5,8,128]{2,1,0:T(8,128)S(1)}, f32[5,8,128]{2,1,0:T(8,128)S(1)}, u32[]{:S(2)}, u32[]{:S(2)}) %collective-permute-start.1) | collective-permute-done | bytes 20512 | tf_op jit(solution)/shard_map/ppermute | solution.py:387
  72.7 0.1 shard_map.79
  72.8 0.0 collective-permute-start.2
  72.8 2.7 %collective-permute-start.3 = (f32[10,8,128]{2,1,0:T(8,128)S(1)}, f32[10,8,128]{2,1,0:T(8,128)S(1)}, u32[]{:S(2)}, u32[]{:S(2)}) collective-permute-start(f32[10,8,128]{2,1,0:T(8,128)S(1)} %get-tuple-element.17), channel_id=1, source_target_pairs={{32,0},{64,32},{96,64},{0,96},{33,1},{65,33},{97,65},{1,97},{34,2}... | collective-permute-start | bytes 122888 | tf_op jit(solution)/shard_map/ppermute | solution.py:397
  75.5 0.1 pad_add_fusion.place_ref
  75.6 1.3 %collective-permute-done.2.from_north_ref = f32[10,8,128]{2,1,0:T(8,128)S(1)} collective-permute-done((f32[10,8,128]{2,1,0:T(8,128)S(1)}, f32[10,8,128]{2,1,0:T(8,128)S(1)}, u32[]{:S(2)}, u32[]{:S(2)}) %collective-permute-start.2) | collective-permute-done | bytes 40992 | tf_op jit(solution)/shard_map/ppermute | solution.py:396
  76.9 0.0 collective-permute-done.3.from_south_ref
  76.9 2.3 %shard_map.80 = (f32[4,128,128]{2,1,0:T(8,128)S(1)}, f32[128,128]{1,0:T(8,128)S(1)}) custom-call(s32[2]{0:T(128)S(1)} %pad_add_fusion.place_ref, f32[5,128,128]{2,1,0:T(8,128)S(1)} %get-tuple-element.11.fields_ref, f32[5,8,128]{2,1,0:T(8,128)S(1)} %collective-permute-done.from_west_ref, f32[5,8,128]{2,1,0:T(8,128)S(1)} %collective-permute-done.1.from_east_ref, ...), custom_call_target="tpu_custom_call" | custom-call | tf_op jit(solution)/shard_map/pallas_call | solution.py:399
  79.2 21.0 %all_to_all.17 = f32[128,1,128]{2,1,0:T(1,128)S(1)} all-to-all(f32[128,1,128]{2,1,0:T(1,128)S(1)} %bitcast.8), channel_id=1, replica_groups=mesh['north'=4,'east'=32] {'north','east'}, dimensions={0} | all-to-all | bytes 131072 | tf_op jit(solution)/shard_map/all_to_all | solution.py:406
  100.2 0.9 shard_map.81
Async XLA Ops:
  1.3 1.0 copy-start
  2.2 0.9 copy-start.1
  3.1 0.9 copy-start.2
  4.0 0.9 copy-start.3
  4.9 0.7 copy-start.4
  68.1 2.3 %collective-permute-start = (f32[5,8,128]{2,1,0:T(8,128)S(1)}, f32[5,8,128]{2,1,0:T(8,128)S(1)}, u32[]{:S(2)}, u32[]{:S(2)}) collective-permute-start(f32[5,8,128]{2,1,0:T(8,128)S(1)} %get-tuple-element.12), channel_id=1, source_target_pairs={{0,1},{1,2},{2,3},{3,4},{4,5},{5,6},{6,7},{7,8},{8,9},{9,10},{10,1... | collective-permute-start | bytes 61448 | tf_op jit(solution)/shard_map/ppermute | solution.py:386
  69.5 3.2 %collective-permute-start.1 = (f32[5,8,128]{2,1,0:T(8,128)S(1)}, f32[5,8,128]{2,1,0:T(8,128)S(1)}, u32[]{:S(2)}, u32[]{:S(2)}) collective-permute-start(f32[5,8,128]{2,1,0:T(8,128)S(1)} %get-tuple-element.13), channel_id=1, source_target_pairs={{1,0},{2,1},{3,2},{4,3},{5,4},{6,5},{7,6},{8,7},{9,8},{10,9},{11,1... | collective-permute-start | bytes 61448 | tf_op jit(solution)/shard_map/ppermute | solution.py:387
  72.8 4.1 %collective-permute-start.2 = (f32[10,8,128]{2,1,0:T(8,128)S(1)}, f32[10,8,128]{2,1,0:T(8,128)S(1)}, u32[]{:S(2)}, u32[]{:S(2)}) collective-permute-start(f32[10,8,128]{2,1,0:T(8,128)S(1)} %get-tuple-element.16), channel_id=1, source_target_pairs={{0,32},{32,64},{64,96},{96,0},{1,33},{33,65},{65,97},{97,1},{2,34}... | collective-permute-start | bytes 122888 | tf_op jit(solution)/shard_map/ppermute | solution.py:396
  72.8 4.1 %collective-permute-start.3 = (f32[10,8,128]{2,1,0:T(8,128)S(1)}, f32[10,8,128]{2,1,0:T(8,128)S(1)}, u32[]{:S(2)}, u32[]{:S(2)}) collective-permute-start(f32[10,8,128]{2,1,0:T(8,128)S(1)} %get-tuple-element.17), channel_id=1, source_target_pairs={{32,0},{64,32},{96,64},{0,96},{33,1},{65,33},{97,65},{1,97},{34,2}... | collective-permute-start | bytes 122888 | tf_op jit(solution)/shard_map/ppermute | solution.py:397

commit v3 on v2

v3 whole, which is shorter than its diff:
```python
import jax
import jax.numpy as jnp
from jax import lax
from jax.experimental import pallas as pl
from jax.experimental.pallas import tpu as pltpu
from jax.sharding import PartitionSpec as P

TR = 128
TC = 128
BLK_DEV = 256
MOST = 4
N_NORTH = 4
N_EAST = 32
TILES = N_NORTH * N_EAST
SHRINK = 1.0 / 64.0
TENSION = 0.75
AXES = ("north", "east")
f32 = jnp.float32
bf16 = jnp.bfloat16

UNITS = 8
GROUPS = TILES * MOST // 128
PAIRS = GROUPS // 2
HALF = 24
WINDOW = 2 * HALF
BANDS = 16
TWO_HOT = 10
SPILL = BANDS * HALF
REACH = 176
STEPS = 128 // UNITS
WINDOWS = -(-127 // WINDOW)


def whole(space=pltpu.VMEM):
    return pl.BlockSpec(memory_space=space)


def row_of(cell):
    return jnp.floor((cell + 0.5) * (1.0 / 127.0))


def sort_lanes(keys):
    lane = lax.broadcasted_iota(jnp.int32, keys.shape, 1)
    size = 2
    while size <= 128:
        gap = size // 2
        while gap >= 1:
            low = (lane & gap) == 0
            other = jnp.take_along_axis(keys, lane ^ gap, axis=1)
            take_min = low == ((lane & size) == 0)
            keys = jnp.where(take_min, jnp.minimum(keys, other), jnp.maximum(keys, other))
            gap //= 2
        size *= 2
    return keys


def route_kernel(dest_hbm, count_ref, cells_hbm, frac_hbm, weight_hbm, height_hbm, out_ref,
                 dest_ref, seen_ref, slot_ref, cells_ref, frac_ref, weight_ref, height_ref, sorted_ref, sems):
    copies = [
        pltpu.make_async_copy(src, dst, sems.at[k])
        for k, (src, dst) in enumerate([
            (dest_hbm, dest_ref), (cells_hbm, cells_ref), (frac_hbm, frac_ref),
            (weight_hbm, weight_ref), (height_hbm, height_ref)])
    ]
    for c in copies:
        c.start()

    def clear(k, _):
        seen_ref[k] = 0
        out_ref[k, 3] = jnp.zeros((MOST, 128), f32)
        return 0

    lax.fori_loop(0, TILES, clear, 0, unroll=8)
    for c in copies:
        c.wait()
    for b in range(BLK_DEV):
        tile = dest_ref[b]
        rank = seen_ref[tile]
        seen_ref[tile] = rank + 1
        slot_ref[b] = rank
    cell = cells_ref[...].astype(f32)
    lane = lax.broadcasted_iota(jnp.int32, cell.shape, 1).astype(f32)
    keys = sort_lanes(row_of(cell) * 128.0 + lane)
    source = (keys - 128.0 * jnp.floor(keys * (1.0 / 128.0))).astype(jnp.int32)
    live = lax.broadcasted_iota(jnp.int32, cell.shape, 0) < count_ref[0]
    weight = jnp.where(live, weight_ref[...], 0.0)
    values = [cell, frac_ref[:, 0, :], frac_ref[:, 1, :], weight, height_ref[...]]
    for f, v in enumerate(values):
        sorted_ref[f] = jnp.take_along_axis(v, source, axis=1)

    for b in range(BLK_DEV):
        tile = dest_ref[b]
        rank = slot_ref[b]
        for f in range(5):
            out_ref[tile, f, pl.ds(rank, 1), :] = sorted_ref[f, b:b + 1, :]


def high_low(value):
    high = value.astype(bf16).astype(f32)
    return [high, value - high]


def build(rank, base, pair, group, by_rank_ref, vals_ref):
    lanes_in = slice(group * 128, group * 128 + 128)
    cell, d, e, mass, height = [by_rank_ref[pair, f, pl.ds(rank, UNITS), lanes_in] for f in range(5)]
    i = row_of(cell)
    j = cell - 127.0 * i
    inner = i - base.astype(f32)
    lower = inner >= float(HALF)
    i_in = jnp.where((inner >= 0.0) & (inner < float(WINDOW)), jnp.where(lower, inner - float(HALF), inner), -100.0)
    place = j + jnp.where(lower, 128.0, 0.0)
    a0, a1, b0, b1 = 1.0 - d, d, 1.0 - e, e
    mh = mass * height
    cols = [mass * b0 * b0, mass * b1 * b1, mass * b0 * b1]
    ends = [mh * b0, mh * b1]
    down, up, mid = [], [], []
    for c in cols:
        down += high_low(c * a1 * a1)
        up += high_low(c * a0 * a0)
        mid += high_low(c * a0 * a1)
    for c in ends:
        down += high_low(c * a1)
        up += high_low(c * a0)
    for k, v in enumerate(down + up + mid + [i_in, place]):
        vals_ref[group, k * UNITS:(k + 1) * UNITS, :] = v
    iota = lax.broadcasted_iota(jnp.int32, (16, 128), 0).astype(f32).astype(bf16)
    zero = jnp.zeros((16, 128), bf16)
    one = jnp.ones((16, 128), bf16)

    def row(k, s):
        return jnp.broadcast_to(vals_ref[group, k * UNITS + s:k * UNITS + s + 1, :], (16, 128))

    eighth = jnp.where(iota < 8.0, iota, iota - 8.0) + 16.0
    first = iota < 8.0
    lefts, rights = [], []
    for s in range(UNITS):
        i_row = row(26, s)
        i_b = i_row.astype(bf16)
        i_next = (i_row + 1.0).astype(bf16)
        at, at_end = iota == i_b, eighth == i_b
        after, after_end = iota == i_next, eighth == i_next
        pieces = []
        for k in range(0, TWO_HOT, 2):
            v1 = [row(k + n, s).astype(bf16) for n in range(2)]
            v0 = [row(TWO_HOT + k + n, s).astype(bf16) for n in range(2)]
            for n in range(2):
                pieces.append(jnp.where(at, v0[n], jnp.where(after, v1[n], zero)))
            pieces.append(jnp.where(at_end, jnp.where(first, v0[0], v0[1]),
                                    jnp.where(after_end, jnp.where(first, v1[0], v1[1]), zero)))
        for k in range(2 * TWO_HOT, 2 * TWO_HOT + BANDS - TWO_HOT, 2):
            v = [row(k + n, s).astype(bf16) for n in range(2)]
            for n in range(2):
                pieces.append(jnp.where(at, v[n], zero))
            pieces.append(jnp.where(at_end, jnp.where(first, v[0], v[1]), zero))
        spill = vals_ref[group, pl.ds(s, 16, stride=UNITS), :]
        pieces.append(jnp.where(i_row == float(HALF - 1), spill, 0.0).astype(bf16))
        lefts.append(jnp.concatenate(pieces, axis=0))
        p_b = row(27, s).astype(bf16)
        rights.append(jnp.concatenate([jnp.where((iota + float(16 * g)) == p_b, one, zero) for g in range(16)], axis=0))
    return lefts, rights


def shifted(a, by, axis):
    return pltpu.roll(a, by % a.shape[axis], axis)


def gather_kernel(place_ref, x_ref, fields_ref, top_ref, bottom_ref, across_ref, beside_ref,
                  by_rank_ref, bounds_ref, limits_ref, items_ref, vals_ref, acc_ref, sem):
    for p in range(PAIRS):
        least, most = [], []
        for g in range(2):
            lanes = slice(g * 128, g * 128 + 128)
            first = (2 * p + g) * 32
            fields = [x_ref[first:first + 32, f].reshape(128, 128).T for f in range(5)]
            live = fields[3] > 0.0
            fields = [jnp.where(live, v, 0.0) for v in fields]
            for f, v in enumerate(fields):
                by_rank_ref[p, f, :, lanes] = v
            i = row_of(fields[0])
            least.append(jnp.where(live, i, 1000.0))
            most.append(jnp.where(live, i, -1.0))
        low = jnp.min(jnp.minimum(least[0], least[1]).T, axis=0, keepdims=True)
        high = jnp.max(jnp.maximum(most[0], most[1]).T, axis=0, keepdims=True)
        bounds_ref[16 * p:16 * p + 8, :] = jnp.broadcast_to(low, (8, 128)).astype(jnp.int32)
        bounds_ref[16 * p + 8:16 * p + 16, :] = jnp.broadcast_to(high, (8, 128)).astype(jnp.int32)
    copy = pltpu.make_async_copy(bounds_ref, limits_ref, sem)
    copy.start()
    acc_ref[...] = jnp.zeros_like(acc_ref)
    copy.wait()

    count = jnp.int32(0)
    for q in range(STEPS):
        for p in range(PAIRS):
            first = limits_ref[16 * p, q * UNITS]
            last = limits_ref[16 * p + 8, q * UNITS + UNITS - 1]
            base = (first // 8) * 8
            for w in range(WINDOWS):
                items_ref[0, count] = q * UNITS
                items_ref[1, count] = base + w * WINDOW
                items_ref[2, count] = p
                count = count + (base + w * WINDOW <= last).astype(jnp.int32)
    items_ref[0, count] = 0
    items_ref[1, count] = 1000
    items_ref[2, count] = 0

    sub = lax.broadcasted_iota(jnp.int32, (8, 128), 0)

    def item(t, half):
        rank = pl.multiple_of(items_ref[0, t], UNITS)
        base = items_ref[1, t]
        lefts, rights = [], []
        for g in range(2):
            more = build(rank, base, items_ref[2, t], g, by_rank_ref, vals_ref.at[half])
            lefts += more[0]
            rights += more[1]
        out = lax.dot_general(
            jnp.concatenate(lefts, axis=1), jnp.concatenate(rights, axis=1),
            (((1,), (1,)), ((), ())), preferred_element_type=f32)
        base = pl.multiple_of(jnp.where(base > 127, 0, base), 8)
        for k in range(0, BANDS, 2):
            for n in range(2):
                for h in range(2):
                    start = (k + n) * REACH + base + h * HALF
                    cols = slice(h * 128, h * 128 + 128)
                    line = k * HALF + 16 * n
                    acc_ref[pl.ds(start, 16), :] += out[line:line + 16, cols]
                    line = k * HALF + 32 + 8 * n
                    acc_ref[pl.ds(start + 16, 8), :] += out[line:line + 8, cols]
        for k in range(TWO_HOT):
            for h in range(2):
                rows = pl.ds(k * REACH + base + (h + 1) * HALF, 8)
                acc_ref[rows, :] += jnp.where(sub == 0, out[SPILL + k:SPILL + k + 1, h * 128:(h + 1) * 128], 0.0)

    def step(c, _):
        item(2 * c, 0)
        item(2 * c + 1, 1)
        return 0

    lax.fori_loop(0, (count + 1) // 2, step, 0)

    def band(k):
        return acc_ref[k * REACH:k * REACH + TR, :]

    def pair(k):
        return band(k) + band(k + 1)

    diag = pair(0) + shifted(pair(2), 1, 1)
    along_east = pair(4)
    rhs = pair(6) + shifted(pair(8), 1, 1)
    along_south = pair(10) + shifted(pair(12), 1, 1)
    cross = pair(14)
    even = place_ref[1] % 2 == 0
    for k, v in enumerate([rhs, diag, along_east, along_south, cross]):
        fields_ref[k] = v
        top_ref[k] = v[0:8]
        bottom_ref[k] = v[120:128]
        t = v.T
        west, east = t[0:8], t[120:128]
        across_ref[k] = jnp.where(even, east, west)
        beside_ref[k] = jnp.where(even, west, east)


def corner_kernel(place_ref, top_ref, bottom_ref, across_ref, beside_ref, to_across_ref, to_beside_ref):
    lane = lax.broadcasted_iota(jnp.int32, (8, 128), 1)
    even_north = place_ref[0] % 2 == 0
    even_east = place_ref[1] % 2 == 0
    for k in range(5):
        a, b = across_ref[k], beside_ref[k]
        w = jnp.where(even_east, b, a)
        e = shifted(jnp.where(even_east, a, b), 64, 1)
        north = jnp.where(lane < 64, w, e)
        south = jnp.where(lane >= 64, w, e)
        top, bottom = top_ref[k], bottom_ref[k]
        to_across_ref[k] = jnp.where(even_north, bottom, top)
        to_beside_ref[k] = jnp.where(even_north, top, bottom)
        to_across_ref[5 + k] = jnp.where(even_north, south, north)
        to_beside_ref[5 + k] = jnp.where(even_north, north, south)


EXT_R = 144
EXT_C = 256


def krylov_kernel(place_ref, fields_ref, across_e_ref, beside_e_ref, across_n_ref, beside_n_ref,
                  basis_ref, moments_ref):
    gn = place_ref[0]
    ge = place_ref[1]
    rows = lax.broadcasted_iota(jnp.int32, (EXT_R, EXT_C), 0)
    cols = lax.broadcasted_iota(jnp.int32, (EXT_R, EXT_C), 1)
    grow = gn * TR + jnp.where(rows < 136, rows, rows - EXT_R)
    gcol = ge * TC + jnp.where(cols < 192, cols, cols - EXT_C)
    inside = (grow >= 0) & (grow < N_NORTH * TR) & (gcol >= 0) & (gcol < N_EAST * TC)

    even_north = gn % 2 == 0
    even_east = ge % 2 == 0
    ext = []
    for k in range(5):
        a, b = across_e_ref[k], beside_e_ref[k]
        w, e = jnp.where(even_east, b, a), jnp.where(even_east, a, b)
        a, b = across_n_ref[k], beside_n_ref[k]
        from_north, from_south = jnp.where(even_north, b, a), jnp.where(even_north, a, b)
        a, b = across_n_ref[5 + k], beside_n_ref[5 + k]
        n, s = jnp.where(even_north, b, a), jnp.where(even_north, a, b)
        zeros = jnp.zeros((112, 128), f32)
        side = jnp.concatenate([e, zeros, w], axis=0).T
        n_e = shifted(n, 64, 1)
        s_e = shifted(s, 64, 1)
        south_side = jnp.concatenate([s_e, zeros, s], axis=0).T
        north_side = jnp.concatenate([n_e, zeros, n], axis=0).T
        left = jnp.concatenate([fields_ref[k], from_south, from_north], axis=0)
        right = jnp.concatenate([side, south_side[0:8], north_side[120:128]], axis=0)
        full = jnp.concatenate([left, right], axis=1)
        ext.append(jnp.where(inside, full, 0.0))
    v0, diag, along_east, along_south, cross = ext

    def laplace(u, u_l, u_r, u_u, u_d):
        return jnp.where(inside, u_l + u_r + u_u + u_d - 4.0 * u, 0.0)

    def operate(u):
        u_r = shifted(u, -1, 1)
        u_l = shifted(u, 1, 1)
        u_d = shifted(u, -1, 0)
        u_u = shifted(u, 1, 0)
        lu = laplace(u, u_l, u_r, u_u, u_d)
        llu = laplace(lu, shifted(lu, 1, 1), shifted(lu, -1, 1), shifted(lu, 1, 0), shifted(lu, -1, 0))
        u_rd = shifted(u_r, -1, 0)
        out = diag * u + along_east * u_r + along_south * u_d + cross * u_rd
        out = out + shifted(along_east * u + cross * u_d, 1, 1)
        out = out + shifted(along_south * u + cross * u_r + shifted(cross * u, 1, 1), 1, 0)
        return (out + (1.0 - TENSION) * llu - TENSION * lu) * SHRINK

    v = [v0]
    for _ in range(3):
        v.append(operate(v[-1]))
    own = [a[0:TR, 0:TC] for a in v]
    for k in range(4):
        basis_ref[k] = own[k]
    pairs = [(0, 0), (0, 1), (1, 1), (1, 2), (2, 2), (2, 3)]
    lane = lax.broadcasted_iota(jnp.int32, (TILES, 128), 1)
    out = jnp.zeros((TILES, 128), f32)
    for k, (p, q) in enumerate(pairs):
        m = jnp.sum(jnp.sum(own[p] * own[q], axis=0, keepdims=True), axis=1, keepdims=True)
        out = jnp.where(lane == k, m, out)
    moments_ref[...] = out


def finish_kernel(moments_ref, basis_ref, surface_ref, residual_ref):
    total = jnp.sum(moments_ref[...], axis=0, keepdims=True)
    m = [total[:, k:k + 1] for k in range(6)]

    def dot(p, q, shift):
        terms = [p[a] * q[b] * m[a + b + shift] for a in range(len(p)) for b in range(len(q))]
        s = terms[0]
        for t in terms[1:]:
            s = s + t
        return s

    one = jnp.ones_like(m[0])
    res = [one]
    direction = [one]
    surf = []
    rr = m[0]
    for it in range(3):
        alpha = rr / dot(direction, direction, 1)
        surf = [(surf[k] if k < len(surf) else 0.0) + alpha * direction[k] for k in range(len(direction))]
        stepped = [jnp.zeros_like(one)] + [alpha * c for c in direction]
        res = [(res[k] if k < len(res) else 0.0) - stepped[k] for k in range(len(stepped))]
        if it < 2:
            fresh = dot(res, res, 0)
            beta = fresh / rr
            direction = [res[k] + (beta * direction[k] if k < len(direction) else 0.0) for k in range(len(res))]
            rr = fresh
    basis = [basis_ref[k] for k in range(4)]
    out = (surf[0] * SHRINK) * basis[0]
    for k in range(1, 3):
        out = out + (surf[k] * SHRINK) * basis[k]
    surface_ref[...] = out
    out = res[0] * basis[0]
    for k in range(1, 4):
        out = out + res[k] * basis[k]
    residual_ref[...] = out


def swaps(count):
    across = [(i, i ^ 1) for i in range(count)]
    beside = [(0, 0), (count - 1, count - 1)]
    for i in range(1, count - 1, 2):
        beside += [(i, i + 1), (i + 1, i)]
    return across, sorted(beside)


def body(destinations, cells, fractions, weights, heights, counts):
    params = pltpu.CompilerParams(vmem_limit_bytes=40 * 1024 * 1024)
    place = jnp.stack([lax.axis_index("north"), lax.axis_index("east")]).astype(jnp.int32)
    block = (BLK_DEV, 128)
    send = pl.pallas_call(
        route_kernel,
        out_shape=jax.ShapeDtypeStruct((TILES, 5, MOST, 128), f32),
        in_specs=[whole(pltpu.HBM), whole(pltpu.SMEM)] + [whole(pltpu.HBM)] * 4,
        out_specs=whole(),
        scratch_shapes=[
            pltpu.SMEM((BLK_DEV,), jnp.int32),
            pltpu.SMEM((TILES,), jnp.int32),
            pltpu.SMEM((BLK_DEV,), jnp.int32),
            pltpu.VMEM(block, jnp.int32),
            pltpu.VMEM((BLK_DEV, 2, 128), f32),
            pltpu.VMEM(block, f32),
            pltpu.VMEM(block, f32),
            pltpu.VMEM((5, BLK_DEV, 128), f32),
            pltpu.SemaphoreType.DMA((5,)),
        ],
        compiler_params=pltpu.CompilerParams(vmem_limit_bytes=60 * 1024 * 1024),
    )(destinations.reshape(BLK_DEV), counts, cells, fractions, weights, heights)
    got = lax.all_to_all(send, AXES, split_axis=0, concat_axis=0, tiled=True)
    strip = jax.ShapeDtypeStruct((5, 8, 128), f32)
    fields, top, bottom, across, beside = pl.pallas_call(
        gather_kernel,
        out_shape=[jax.ShapeDtypeStruct((5, TR, TC), f32)] + [strip] * 4,
        in_specs=[whole(pltpu.SMEM), whole()],
        out_specs=[whole()] * 5,
        scratch_shapes=[
            pltpu.VMEM((PAIRS, 5, 128, 256), f32),
            pltpu.VMEM((16 * PAIRS, 128), jnp.int32),
            pltpu.SMEM((16 * PAIRS, 128), jnp.int32),
            pltpu.SMEM((3, PAIRS * STEPS * WINDOWS + 8), jnp.int32),
            pltpu.VMEM((2, 2, 28 * UNITS, 128), f32),
            pltpu.VMEM((BANDS * REACH, 128), f32),
            pltpu.SemaphoreType.DMA,
        ],
        compiler_params=params,
    )(place, got)
    east_across, east_beside = swaps(N_EAST)
    north_across, north_beside = swaps(N_NORTH)
    beside_e = lax.ppermute(beside, "east", east_beside)
    across_e = lax.ppermute(across, "east", east_across)
    message = jax.ShapeDtypeStruct((10, 8, 128), f32)
    to_across, to_beside = pl.pallas_call(
        corner_kernel,
        out_shape=[message] * 2,
        in_specs=[whole(pltpu.SMEM)] + [whole()] * 4,
        out_specs=[whole()] * 2,
        compiler_params=params,
    )(place, top, bottom, across_e, beside_e)
    beside_n = lax.ppermute(to_beside, "north", north_beside)
    across_n = lax.ppermute(to_across, "north", north_across)
    basis, moments = pl.pallas_call(
        krylov_kernel,
        out_shape=[jax.ShapeDtypeStruct((4, TR, TC), f32), jax.ShapeDtypeStruct((TILES, 128), f32)],
        in_specs=[whole(pltpu.SMEM)] + [whole()] * 5,
        out_specs=[whole()] * 2,
        compiler_params=params,
    )(place, fields, across_e, beside_e, across_n, beside_n)
    spread = lax.all_to_all(moments, AXES, split_axis=0, concat_axis=0, tiled=True)
    return pl.pallas_call(
        finish_kernel,
        out_shape=[jax.ShapeDtypeStruct((TR, TC), f32)] * 2,
        in_specs=[whole()] * 2,
        out_specs=[whole()] * 2,
        compiler_params=params,
    )(spread, basis)


def solution(mesh):
    return jax.shard_map(
        body,
        mesh=mesh,
        in_specs=(
            P(AXES, None),
            P(AXES, None),
            P(AXES, None, None),
            P(AXES, None),
            P(AXES, None),
            P(AXES),
        ),
        out_specs=(P("north", "east"), P("north", "east")),
        check_vma=False,
    )
```

time: 101 us -> 93 us (0.921)
  blocking collectives: 53.7 us -> 18.6 us
  waiting for transfers between devices: 4.46 us -> 26.7 us
  starting transfers between devices: 4.12 us -> 16 us
  local copies, waits for them, and re-layouts: 4.33 us -> 0 us
  Pallas kernels: 33.1 us -> 30 us
    all_to_all x1 -> x0, blocking collectives: 32.7 us -> none  [body(): got = lax.all_to_all(send, AXES, split_axis=0, concat_axis=0, tiled=True)]
    all_to_all x0 -> x1, waiting for transfers between devices: none -> 21.6 us  [body(): got = lax.all_to_all(send, AXES, split_axis=0, concat_axis=0, tiled=True)]
    all_to_all x0 -> x1, starting transfers between devices: none -> 11.5 us  [body(): got = lax.all_to_all(send, AXES, split_axis=0, concat_axis=0, tiled=True)]
    unnamed x10 -> x0, local copies, waits for them, and re-layouts: 4.33 us -> none
    all_to_all x1, blocking collectives: 21 us -> 18.6 us  [body(): lax.all_to_all(moments, AXES, split_axis=0, concat_axis=0, tiled=True)]
    pallas_call x1, Pallas kernels: 23.3 us -> 21 us  [body(): pl.pallas_call(gather_kernel, out_shape=[jax.ShapeDtypeStruct((5, TR, TC)...]
    pallas_call x1, Pallas kernels: 6.51 us -> 5.21 us  [body(): pl.pallas_call(route_kernel, out_shape=jax.ShapeDtypeStruct((TILES, 5, MO...]
  transfers between devices with their start and end apart: 4 -> 5, of which waited for: 3 -> 3; matrix products, arithmetic and copies ran while one was open for 0% -> 0% of each run, Pallas kernels for 0% -> 0%
where the time goes in v3:
time: 93 us; the launch traced here: 92.8 us
  Pallas kernels  30 us (32%)
  waiting for transfers between devices  26.7 us (29%)
  blocking collectives  18.6 us (20%)
  starting transfers between devices  16 us (17%)
  between operations  1.34 us (1%)
    all_to_all x1, waiting for transfers between devices, body(): got = lax.all_to_all(send, AXES, split_axis=0, concat_axis=0, tiled=True)  21.6 us
    pallas_call x1, Pallas kernels, body(): pl.pallas_call(gather_kernel, out_shape=[jax.ShapeDtypeStruct((5, TR, TC)...  21 us
    all_to_all x1, blocking collectives, body(): lax.all_to_all(moments, AXES, split_axis=0, concat_axis=0, tiled=True)  18.6 us
    all_to_all x1, starting transfers between devices, body(): got = lax.all_to_all(send, AXES, split_axis=0, concat_axis=0, tiled=True)  11.5 us
    pallas_call x1, Pallas kernels, body(): pl.pallas_call(route_kernel, out_shape=jax.ShapeDtypeStruct((TILES, 5, MO...  5.21 us
    ppermute x1, waiting for transfers between devices, body(): beside_e = lax.ppermute(beside, 'east', east_beside)  3.43 us
    pallas_call x1, Pallas kernels, body(): pl.pallas_call(krylov_kernel, out_shape=[jax.ShapeDtypeStruct((4, TR, TC)...  2.35 us
    ppermute x1, starting transfers between devices, body(): beside_e = lax.ppermute(beside, 'east', east_beside)  1.94 us
  transfers between devices with their start and end apart: 5, of which 3 were waited for; matrix products, arithmetic and copies ran while one was open for 0% of the time, Pallas kernels for 0%

profile of v3, /device:TPU:1, one launch (start us, length us, event | category | flops | bytes accessed | tf_op | source)
XLA Modules:
  0.0 92.8 jit_solution(13860695508547137931)
XLA Ops:
  1.3 5.2 %shard_map.77 = f32[128,5,4,128]{3,2,1,0:T(4,128)} custom-call(s32[256]{0:T(256)} %bitcast.9, s32[1]{0:T(128)S(6)} %copy.9.count_ref, s32[256,128]{1,0:T(8,128)} %cells_hbm.1, f32[256,2,128]{2,1,0:T(2,128)} %frac_hbm.1, f32[256,128]{1,0:T(8,128)} %weight_hbm.1, f32[256,128]{1,0:T(8,128)} %height_hbm.1), custom_call_target="tpu_custom_call" | custom-call | tf_op jit(solution)/shard_map/pallas_call | solution.py:396
  6.5 11.5 %all-to-all-start = ((f32[128,5,4,128]{3,2,1,0:T(4,128)}), f32[128,5,4,128]{3,2,1,0:T(4,128)S(1)}, u32[]{:S(2)}, u32[]{:S(2)}) async-start(f32[128,5,4,128]{3,2,1,0:T(4,128)} %shard_map.77), calls=%async_computation | async-start | bytes 2621440 | tf_op jit(solution)/shard_map/all_to_all | solution.py:414
  18.0 0.1 pad_add_fusion.place_ref
  18.1 21.6 %all-to-all-done.x_ref = f32[128,5,4,128]{3,2,1,0:T(4,128)S(1)} async-done(((f32[128,5,4,128]{3,2,1,0:T(4,128)}), f32[128,5,4,128]{3,2,1,0:T(4,128)S(1)}, u32[]{:S(2)}, u32[]{:S(2)}) %all-to-all-start) | async-done | bytes 1310752 | tf_op jit(solution)/shard_map/all_to_all | solution.py:414
  39.7 21.0 %shard_map.78 = (f32[5,128,128]{2,1,0:T(8,128)S(1)}, f32[5,8,128]{2,1,0:T(8,128)S(1)}, f32[5,8,128]{2,1,0:T(8,128)S(1)}, f32[5,8,128]{2,1,0:T(8,128)S(1)}, f32[5,8,128]{2,1,0:T(8,128)S(1)}) custom-call(s32[2]{0:T(128)S(1)} %pad_add_fusion.place_ref, f32[128,5,4,128]{3,2,1,0:T(4,128)S(1)} %all-to-all-done.x_ref), custom_call_target="tpu_custom_call" | custom-call | tf_op jit(solution)/shard_map/pallas_call | solution.py:416
  60.6 1.4 %collective-permute-start = (f32[5,8,128]{2,1,0:T(8,128)S(1)}, f32[5,8,128]{2,1,0:T(8,128)S(1)}, u32[]{:S(2)}, u32[]{:S(2)}) collective-permute-start(f32[5,8,128]{2,1,0:T(8,128)S(1)} %get-tuple-element.12), channel_id=1, source_target_pairs={{0,1},{1,0},{2,3},{3,2},{4,5},{5,4},{6,7},{7,6},{8,9},{9,8},{10,11... | collective-permute-start | bytes 61448 | tf_op jit(solution)/shard_map/ppermute | solution.py:435
  62.0 1.9 %collective-permute-start.1 = (f32[5,8,128]{2,1,0:T(8,128)S(1)}, f32[5,8,128]{2,1,0:T(8,128)S(1)}, u32[]{:S(2)}, u32[]{:S(2)}) collective-permute-start(f32[5,8,128]{2,1,0:T(8,128)S(1)} %get-tuple-element.13), channel_id=1, source_target_pairs={{0,0},{1,2},{2,1},{3,4},{4,3},{5,6},{6,5},{7,8},{8,7},{9,10},{10,9... | collective-permute-start | bytes 61448 | tf_op jit(solution)/shard_map/ppermute | solution.py:434
  64.0 0.0 collective-permute-done.across_ref.across_e_ref
  64.0 3.4 %collective-permute-done.1.beside_ref.beside_e_ref = f32[5,8,128]{2,1,0:T(8,128)S(1)} collective-permute-done((f32[5,8,128]{2,1,0:T(8,128)S(1)}, f32[5,8,128]{2,1,0:T(8,128)S(1)}, u32[]{:S(2)}, u32[]{:S(2)}) %collective-permute-start.1) | collective-permute-done | bytes 20512 | tf_op jit(solution)/shard_map/ppermute | solution.py:434
  67.4 0.6 shard_map.79
  68.0 0.6 collective-permute-start.2
  68.6 0.7 collective-permute-start.3
  69.3 1.7 %collective-permute-done.2.across_n_ref = f32[10,8,128]{2,1,0:T(8,128)S(1)} collective-permute-done((f32[10,8,128]{2,1,0:T(8,128)S(1)}, f32[10,8,128]{2,1,0:T(8,128)S(1)}, u32[]{:S(2)}, u32[]{:S(2)}) %collective-permute-start.2) | collective-permute-done | bytes 40992 | tf_op jit(solution)/shard_map/ppermute | solution.py:445
  70.9 0.0 collective-permute-done.3.beside_n_ref
  70.9 2.3 %shard_map.80 = (f32[4,128,128]{2,1,0:T(8,128)S(1)}, f32[128,128]{1,0:T(8,128)S(1)}) custom-call(s32[2]{0:T(128)S(1)} %pad_add_fusion.place_ref, f32[5,128,128]{2,1,0:T(8,128)S(1)} %get-tuple-element.11.fields_ref, f32[5,8,128]{2,1,0:T(8,128)S(1)} %collective-permute-done.across_ref.across_e_ref, ...), custom_call_target="tpu_custom_call" | custom-call | tf_op jit(solution)/shard_map/pallas_call | solution.py:446
  73.3 18.6 %all_to_all.16 = f32[128,1,128]{2,1,0:T(1,128)S(1)} all-to-all(f32[128,1,128]{2,1,0:T(1,128)S(1)} %bitcast.8), channel_id=1, replica_groups=mesh['north'=4,'east'=32] {'north','east'}, dimensions={0} | all-to-all | bytes 131072 | tf_op jit(solution)/shard_map/all_to_all | solution.py:453
  91.9 0.9 shard_map.81
Async XLA Ops:
  6.5 33.2 %all-to-all-start = ((f32[128,5,4,128]{3,2,1,0:T(4,128)}), f32[128,5,4,128]{3,2,1,0:T(4,128)S(1)}, u32[]{:S(2)}, u32[]{:S(2)}) async-start(f32[128,5,4,128]{3,2,1,0:T(4,128)} %shard_map.77), calls=%async_computation | async-start | bytes 2621440 | tf_op jit(solution)/shard_map/all_to_all | solution.py:414
  60.6 3.3 %collective-permute-start = (f32[5,8,128]{2,1,0:T(8,128)S(1)}, f32[5,8,128]{2,1,0:T(8,128)S(1)}, u32[]{:S(2)}, u32[]{:S(2)}) collective-permute-start(f32[5,8,128]{2,1,0:T(8,128)S(1)} %get-tuple-element.12), channel_id=1, source_target_pairs={{0,1},{1,0},{2,3},{3,2},{4,5},{5,4},{6,7},{7,6},{8,9},{9,8},{10,11... | collective-permute-start | bytes 61448 | tf_op jit(solution)/shard_map/ppermute | solution.py:435
  62.0 5.4 %collective-permute-start.1 = (f32[5,8,128]{2,1,0:T(8,128)S(1)}, f32[5,8,128]{2,1,0:T(8,128)S(1)}, u32[]{:S(2)}, u32[]{:S(2)}) collective-permute-start(f32[5,8,128]{2,1,0:T(8,128)S(1)} %get-tuple-element.13), channel_id=1, source_target_pairs={{0,0},{1,2},{2,1},{3,4},{4,3},{5,6},{6,5},{7,8},{8,7},{9,10},{10,9... | collective-permute-start | bytes 61448 | tf_op jit(solution)/shard_map/ppermute | solution.py:434
  68.0 2.9 %collective-permute-start.2 = (f32[10,8,128]{2,1,0:T(8,128)S(1)}, f32[10,8,128]{2,1,0:T(8,128)S(1)}, u32[]{:S(2)}, u32[]{:S(2)}) collective-permute-start(f32[10,8,128]{2,1,0:T(8,128)S(1)} %get-tuple-element.16), channel_id=1, source_target_pairs={{0,32},{32,0},{64,96},{96,64},{1,33},{33,1},{65,97},{97,65},{2,34}... | collective-permute-start | bytes 122888 | tf_op jit(solution)/shard_map/ppermute | solution.py:445
  68.6 2.3 %collective-permute-start.3 = (f32[10,8,128]{2,1,0:T(8,128)S(1)}, f32[10,8,128]{2,1,0:T(8,128)S(1)}, u32[]{:S(2)}, u32[]{:S(2)}) collective-permute-start(f32[10,8,128]{2,1,0:T(8,128)S(1)} %get-tuple-element.17), channel_id=1, source_target_pairs={{0,0},{32,64},{64,32},{96,96},{1,1},{33,65},{65,33},{97,97},{2,2},... | collective-permute-start | bytes 122888 | tf_op jit(solution)/shard_map/ppermute | solution.py:444

commit v4 on v3

--- a/solution.py
+++ b/solution.py
@@ -71,7 +71,7 @@
         return 0
 
     lax.fori_loop(0, TILES, clear, 0, unroll=8)
-    for c in copies:
+    for c in copies[:2]:
         c.wait()
     for b in range(BLK_DEV):
         tile = dest_ref[b]
@@ -82,6 +82,8 @@
     lane = lax.broadcasted_iota(jnp.int32, cell.shape, 1).astype(f32)
     keys = sort_lanes(row_of(cell) * 128.0 + lane)
     source = (keys - 128.0 * jnp.floor(keys * (1.0 / 128.0))).astype(jnp.int32)
+    for c in copies[2:]:
+        c.wait()
     live = lax.broadcasted_iota(jnp.int32, cell.shape, 0) < count_ref[0]
     weight = jnp.where(live, weight_ref[...], 0.0)
     values = [cell, frac_ref[:, 0, :], frac_ref[:, 1, :], weight, height_ref[...]]
@@ -231,12 +233,18 @@
                 rows = pl.ds(k * REACH + base + (h + 1) * HALF, 8)
                 acc_ref[rows, :] += jnp.where(sub == 0, out[SPILL + k:SPILL + k + 1, h * 128:(h + 1) * 128], 0.0)
 
-    def step(c, _):
-        item(2 * c, 0)
-        item(2 * c + 1, 1)
+    def four(c, _):
+        for n in range(8):
+            item(8 * c + n, n)
         return 0
 
-    lax.fori_loop(0, (count + 1) // 2, step, 0)
+    def two(c, _):
+        for n in range(2):
+            item(2 * c + n, n)
+        return 0
+
+    lax.fori_loop(0, count // 8, four, 0)
+    lax.fori_loop(4 * (count // 8), (count + 1) // 2, two, 0)
 
     def band(k):
         return acc_ref[k * REACH:k * REACH + TR, :]
@@ -249,7 +257,7 @@
     rhs = pair(6) + shifted(pair(8), 1, 1)
     along_south = pair(10) + shifted(pair(12), 1, 1)
     cross = pair(14)
-    even = place_ref[1] % 2 == 0
+    even = (place_ref[8:16, :] & 1) == 0
     for k, v in enumerate([rhs, diag, along_east, along_south, cross]):
         fields_ref[k] = v
         top_ref[k] = v[0:8]
@@ -262,8 +270,8 @@
 
 def corner_kernel(place_ref, top_ref, bottom_ref, across_ref, beside_ref, to_across_ref, to_beside_ref):
     lane = lax.broadcasted_iota(jnp.int32, (8, 128), 1)
-    even_north = place_ref[0] % 2 == 0
-    even_east = place_ref[1] % 2 == 0
+    even_north = (place_ref[0:8, :] & 1) == 0
+    even_east = (place_ref[8:16, :] & 1) == 0
     for k in range(5):
         a, b = across_ref[k], beside_ref[k]
         w = jnp.where(even_east, b, a)
@@ -283,16 +291,18 @@
 
 def krylov_kernel(place_ref, fields_ref, across_e_ref, beside_e_ref, across_n_ref, beside_n_ref,
                   basis_ref, moments_ref):
-    gn = place_ref[0]
-    ge = place_ref[1]
+    north, east = place_ref[0:8, :], place_ref[8:16, :]
+    gn = jnp.concatenate([jnp.concatenate([north] * (EXT_R // 8), axis=0)] * 2, axis=1)
+    ge = jnp.concatenate([jnp.concatenate([east] * (EXT_R // 8), axis=0)] * 2, axis=1)
     rows = lax.broadcasted_iota(jnp.int32, (EXT_R, EXT_C), 0)
     cols = lax.broadcasted_iota(jnp.int32, (EXT_R, EXT_C), 1)
     grow = gn * TR + jnp.where(rows < 136, rows, rows - EXT_R)
     gcol = ge * TC + jnp.where(cols < 192, cols, cols - EXT_C)
     inside = (grow >= 0) & (grow < N_NORTH * TR) & (gcol >= 0) & (gcol < N_EAST * TC)
 
-    even_north = gn % 2 == 0
-    even_east = ge % 2 == 0
+    even_north = (north & 1) == 0
+    even_east = (east & 1) == 0
+    lane = lax.broadcasted_iota(jnp.int32, (8, 128), 1)
     ext = []
     for k in range(5):
         a, b = across_e_ref[k], beside_e_ref[k]
@@ -301,14 +311,15 @@
         from_north, from_south = jnp.where(even_north, b, a), jnp.where(even_north, a, b)
         a, b = across_n_ref[5 + k], beside_n_ref[5 + k]
         n, s = jnp.where(even_north, b, a), jnp.where(even_north, a, b)
-        zeros = jnp.zeros((112, 128), f32)
-        side = jnp.concatenate([e, zeros, w], axis=0).T
-        n_e = shifted(n, 64, 1)
-        s_e = shifted(s, 64, 1)
-        south_side = jnp.concatenate([s_e, zeros, s], axis=0).T
-        north_side = jnp.concatenate([n_e, zeros, n], axis=0).T
+        corner_w = jnp.where(lane < 64, s, n)
+        corner_e = jnp.where(lane < 64, shifted(s, 64, 1), shifted(n, 64, 1))
+        sides = jnp.concatenate([e, corner_e, jnp.zeros((96, 128), f32), corner_w, w], axis=0).T
+
+        def ends(rows):
+            return jnp.where(lane < 64, shifted(rows, -8, 1), shifted(rows, 8, 1))
+
         left = jnp.concatenate([fields_ref[k], from_south, from_north], axis=0)
-        right = jnp.concatenate([side, south_side[0:8], north_side[120:128]], axis=0)
+        right = jnp.concatenate([sides, ends(sides[0:8]), ends(sides[120:128])], axis=0)
         full = jnp.concatenate([left, right], axis=1)
         ext.append(jnp.where(inside, full, 0.0))
     v0, diag, along_east, along_south, cross = ext
@@ -391,11 +402,12 @@
 
 def body(destinations, cells, fractions, weights, heights, counts):
     params = pltpu.CompilerParams(vmem_limit_bytes=40 * 1024 * 1024)
-    place = jnp.stack([lax.axis_index("north"), lax.axis_index("east")]).astype(jnp.int32)
+    row = lax.broadcasted_iota(jnp.int32, (16, 128), 0)
+    place = jnp.where(row < 8, lax.axis_index("north"), lax.axis_index("east")).astype(jnp.int32)
     block = (BLK_DEV, 128)
     send = pl.pallas_call(
         route_kernel,
-        out_shape=jax.ShapeDtypeStruct((TILES, 5, MOST, 128), f32),
+        out_shape=pltpu.VMEM((TILES, 5, MOST, 128), f32),
         in_specs=[whole(pltpu.HBM), whole(pltpu.SMEM)] + [whole(pltpu.HBM)] * 4,
         out_specs=whole(),
         scratch_shapes=[
@@ -409,21 +421,21 @@
             pltpu.VMEM((5, BLK_DEV, 128), f32),
             pltpu.SemaphoreType.DMA((5,)),
         ],
-        compiler_params=pltpu.CompilerParams(vmem_limit_bytes=60 * 1024 * 1024),
+        compiler_params=pltpu.CompilerParams(vmem_limit_bytes=62_050_000),
     )(destinations.reshape(BLK_DEV), counts, cells, fractions, weights, heights)
     got = lax.all_to_all(send, AXES, split_axis=0, concat_axis=0, tiled=True)
     strip = jax.ShapeDtypeStruct((5, 8, 128), f32)
     fields, top, bottom, across, beside = pl.pallas_call(
         gather_kernel,
         out_shape=[jax.ShapeDtypeStruct((5, TR, TC), f32)] + [strip] * 4,
-        in_specs=[whole(pltpu.SMEM), whole()],
+        in_specs=[whole()] * 2,
         out_specs=[whole()] * 5,
         scratch_shapes=[
             pltpu.VMEM((PAIRS, 5, 128, 256), f32),
             pltpu.VMEM((16 * PAIRS, 128), jnp.int32),
             pltpu.SMEM((16 * PAIRS, 128), jnp.int32),
             pltpu.SMEM((3, PAIRS * STEPS * WINDOWS + 8), jnp.int32),
-            pltpu.VMEM((2, 2, 28 * UNITS, 128), f32),
+            pltpu.VMEM((8, 2, 28 * UNITS, 128), f32),
             pltpu.VMEM((BANDS * REACH, 128), f32),
             pltpu.SemaphoreType.DMA,
         ],
@@ -437,7 +449,7 @@
     to_across, to_beside = pl.pallas_call(
         corner_kernel,
         out_shape=[message] * 2,
-        in_specs=[whole(pltpu.SMEM)] + [whole()] * 4,
+        in_specs=[whole()] * 5,
         out_specs=[whole()] * 2,
         compiler_params=params,
     )(place, top, bottom, across_e, beside_e)
@@ -446,7 +458,7 @@
     basis, moments = pl.pallas_call(
         krylov_kernel,
         out_shape=[jax.ShapeDtypeStruct((4, TR, TC), f32), jax.ShapeDtypeStruct((TILES, 128), f32)],
-        in_specs=[whole(pltpu.SMEM)] + [whole()] * 5,
+        in_specs=[whole()] * 6,
         out_specs=[whole()] * 2,
         compiler_params=params,
     )(place, fields, across_e, beside_e, across_n, beside_n)

time: 93 us -> 88.5 us (0.952)
  Pallas kernels: 30 us -> 25.4 us
  blocking collectives: 18.6 us -> 17 us
    pallas_call x1, Pallas kernels: 21 us -> 17.9 us  [body(): pl.pallas_call(gather_kernel, out_shape=[jax.ShapeDtypeStruct((5, TR, TC)...]
    all_to_all x1, blocking collectives: 18.6 us -> 17 us  [body(): lax.all_to_all(moments, AXES, split_axis=0, concat_axis=0, tiled=True)]
    ppermute x1, starting transfers between devices: 1.39 us -> 2.53 us  [body(): across_e = lax.ppermute(across, 'east', east_across)]
where the time goes in v4:
time: 88.5 us; the launch traced here: 87.4 us
  waiting for transfers between devices  27 us (31%)
  Pallas kernels  25.4 us (29%)
  blocking collectives  17 us (19%)
  starting transfers between devices  16.6 us (19%)
  between operations  1.35 us (2%)
    all_to_all x1, waiting for transfers between devices, body(): got = lax.all_to_all(send, AXES, split_axis=0, concat_axis=0, tiled=True)  21.7 us
    pallas_call x1, Pallas kernels, body(): pl.pallas_call(gather_kernel, out_shape=[jax.ShapeDtypeStruct((5, TR, TC)...  17.9 us
    all_to_all x1, blocking collectives, body(): lax.all_to_all(moments, AXES, split_axis=0, concat_axis=0, tiled=True)  17 us
    all_to_all x1, starting transfers between devices, body(): got = lax.all_to_all(send, AXES, split_axis=0, concat_axis=0, tiled=True)  11.5 us
    pallas_call x1, Pallas kernels, body(): pl.pallas_call(route_kernel, out_shape=pltpu.VMEM((TILES, 5, MOST, 128),...  4.87 us
    ppermute x1, waiting for transfers between devices, body(): beside_e = lax.ppermute(beside, 'east', east_beside)  3.16 us
    ppermute x1, starting transfers between devices, body(): across_e = lax.ppermute(across, 'east', east_across)  2.53 us
    ppermute x1, waiting for transfers between devices, body(): across_n = lax.ppermute(to_across, 'north', north_across)  2.17 us
  transfers between devices with their start and end apart: 5, of which 3 were waited for; matrix products, arithmetic and copies ran while one was open for 0% of the time, Pallas kernels for 0%

profile of v4, /device:TPU:1, one launch (start us, length us, event | category | flops | bytes accessed | tf_op | source)
XLA Modules:
  0.0 87.4 jit_solution(13111128027950757112)
XLA Ops:
  1.3 4.9 %shard_map.77 = f32[128,5,4,128]{3,2,1,0:T(4,128)} custom-call(s32[256]{0:T(256)} %bitcast.7, s32[1]{0:T(128)S(6)} %copy.9.count_ref, s32[256,128]{1,0:T(8,128)} %cells_hbm.1, f32[256,2,128]{2,1,0:T(2,128)} %frac_hbm.1, f32[256,128]{1,0:T(8,128)} %weight_hbm.1, f32[256,128]{1,0:T(8,128)} %height_hbm.1), custom_call_target="tpu_custom_call" | custom-call | tf_op jit(solution)/shard_map/pallas_call | solution.py:408
  6.2 11.5 %all-to-all-start = ((f32[128,5,4,128]{3,2,1,0:T(4,128)}), f32[128,5,4,128]{3,2,1,0:T(4,128)S(1)}, u32[]{:S(2)}, u32[]{:S(2)}) async-start(f32[128,5,4,128]{3,2,1,0:T(4,128)} %shard_map.77), calls=%async_computation | async-start | bytes 2621440 | tf_op jit(solution)/shard_map/all_to_all | solution.py:426
  17.7 21.7 %all-to-all-done.x_ref = f32[128,5,4,128]{3,2,1,0:T(4,128)S(1)} async-done(((f32[128,5,4,128]{3,2,1,0:T(4,128)}), f32[128,5,4,128]{3,2,1,0:T(4,128)S(1)}, u32[]{:S(2)}, u32[]{:S(2)}) %all-to-all-start) | async-done | bytes 1310752 | tf_op jit(solution)/shard_map/all_to_all | solution.py:426
  39.3 0.1 iota.7.place_ref
  39.4 17.9 %shard_map.78 = (f32[5,128,128]{2,1,0:T(8,128)S(1)}, f32[5,8,128]{2,1,0:T(8,128)S(1)}, f32[5,8,128]{2,1,0:T(8,128)S(1)}, f32[5,8,128]{2,1,0:T(8,128)S(1)}, f32[5,8,128]{2,1,0:T(8,128)S(1)}) custom-call(s32[16,128]{1,0:T(8,128)S(1)} %iota.7.place_ref, f32[128,5,4,128]{3,2,1,0:T(4,128)S(1)} %all-to-all-done.x_ref), custom_call_target="tpu_custom_call" | custom-call | tf_op jit(solution)/shard_map/pallas_call | solution.py:428
  57.3 2.5 %collective-permute-start = (f32[5,8,128]{2,1,0:T(8,128)S(1)}, f32[5,8,128]{2,1,0:T(8,128)S(1)}, u32[]{:S(2)}, u32[]{:S(2)}) collective-permute-start(f32[5,8,128]{2,1,0:T(8,128)S(1)} %get-tuple-element.12), channel_id=1, source_target_pairs={{0,1},{1,0},{2,3},{3,2},{4,5},{5,4},{6,7},{7,6},{8,9},{9,8},{10,11... | collective-permute-start | bytes 61448 | tf_op jit(solution)/shard_map/ppermute | solution.py:447
  59.8 1.9 %collective-permute-start.1 = (f32[5,8,128]{2,1,0:T(8,128)S(1)}, f32[5,8,128]{2,1,0:T(8,128)S(1)}, u32[]{:S(2)}, u32[]{:S(2)}) collective-permute-start(f32[5,8,128]{2,1,0:T(8,128)S(1)} %get-tuple-element.13), channel_id=1, source_target_pairs={{0,0},{1,2},{2,1},{3,4},{4,3},{5,6},{6,5},{7,8},{8,7},{9,10},{10,9... | collective-permute-start | bytes 61448 | tf_op jit(solution)/shard_map/ppermute | solution.py:446
  61.7 0.0 collective-permute-done.across_ref.across_e_ref
  61.7 3.2 %collective-permute-done.1.beside_ref.beside_e_ref = f32[5,8,128]{2,1,0:T(8,128)S(1)} collective-permute-done((f32[5,8,128]{2,1,0:T(8,128)S(1)}, f32[5,8,128]{2,1,0:T(8,128)S(1)}, u32[]{:S(2)}, u32[]{:S(2)}) %collective-permute-start.1) | collective-permute-done | bytes 20512 | tf_op jit(solution)/shard_map/ppermute | solution.py:446
  64.9 0.1 shard_map.79
  65.0 0.0 collective-permute-start.2
  65.0 0.7 collective-permute-start.3
  65.7 2.2 %collective-permute-done.2.across_n_ref = f32[10,8,128]{2,1,0:T(8,128)S(1)} collective-permute-done((f32[10,8,128]{2,1,0:T(8,128)S(1)}, f32[10,8,128]{2,1,0:T(8,128)S(1)}, u32[]{:S(2)}, u32[]{:S(2)}) %collective-permute-start.2) | collective-permute-done | bytes 40992 | tf_op jit(solution)/shard_map/ppermute | solution.py:457
  67.9 0.0 collective-permute-done.3.beside_n_ref
  67.9 1.7 %shard_map.80 = (f32[4,128,128]{2,1,0:T(8,128)S(1)}, f32[128,128]{1,0:T(8,128)S(1)}) custom-call(s32[16,128]{1,0:T(8,128)S(1)} %iota.7.place_ref, f32[5,128,128]{2,1,0:T(8,128)S(1)} %get-tuple-element.11.fields_ref, f32[5,8,128]{2,1,0:T(8,128)S(1)} %collective-permute-done.across_ref.across_e_ref, ...), custom_call_target="tpu_custom_call" | custom-call | tf_op jit(solution)/shard_map/pallas_call | solution.py:458
  69.6 17.0 %all_to_all.16 = f32[128,1,128]{2,1,0:T(1,128)S(1)} all-to-all(f32[128,1,128]{2,1,0:T(1,128)S(1)} %bitcast.6), channel_id=1, replica_groups=mesh['north'=4,'east'=32] {'north','east'}, dimensions={0} | all-to-all | bytes 131072 | tf_op jit(solution)/shard_map/all_to_all | solution.py:465
  86.6 0.9 shard_map.81
  (1 shorter events, 0.0 us)
Async XLA Ops:
  6.2 33.2 %all-to-all-start = ((f32[128,5,4,128]{3,2,1,0:T(4,128)}), f32[128,5,4,128]{3,2,1,0:T(4,128)S(1)}, u32[]{:S(2)}, u32[]{:S(2)}) async-start(f32[128,5,4,128]{3,2,1,0:T(4,128)} %shard_map.77), calls=%async_computation | async-start | bytes 2621440 | tf_op jit(solution)/shard_map/all_to_all | solution.py:426
  57.3 4.5 %collective-permute-start = (f32[5,8,128]{2,1,0:T(8,128)S(1)}, f32[5,8,128]{2,1,0:T(8,128)S(1)}, u32[]{:S(2)}, u32[]{:S(2)}) collective-permute-start(f32[5,8,128]{2,1,0:T(8,128)S(1)} %get-tuple-element.12), channel_id=1, source_target_pairs={{0,1},{1,0},{2,3},{3,2},{4,5},{5,4},{6,7},{7,6},{8,9},{9,8},{10,11... | collective-permute-start | bytes 61448 | tf_op jit(solution)/shard_map/ppermute | solution.py:447
  59.8 5.1 %collective-permute-start.1 = (f32[5,8,128]{2,1,0:T(8,128)S(1)}, f32[5,8,128]{2,1,0:T(8,128)S(1)}, u32[]{:S(2)}, u32[]{:S(2)}) collective-permute-start(f32[5,8,128]{2,1,0:T(8,128)S(1)} %get-tuple-element.13), channel_id=1, source_target_pairs={{0,0},{1,2},{2,1},{3,4},{4,3},{5,6},{6,5},{7,8},{8,7},{9,10},{10,9... | collective-permute-start | bytes 61448 | tf_op jit(solution)/shard_map/ppermute | solution.py:446
  65.0 2.9 %collective-permute-start.2 = (f32[10,8,128]{2,1,0:T(8,128)S(1)}, f32[10,8,128]{2,1,0:T(8,128)S(1)}, u32[]{:S(2)}, u32[]{:S(2)}) collective-permute-start(f32[10,8,128]{2,1,0:T(8,128)S(1)} %get-tuple-element.16), channel_id=1, source_target_pairs={{0,32},{32,0},{64,96},{96,64},{1,33},{33,1},{65,97},{97,65},{2,34}... | collective-permute-start | bytes 122888 | tf_op jit(solution)/shard_map/ppermute | solution.py:457
  65.0 2.8 %collective-permute-start.3 = (f32[10,8,128]{2,1,0:T(8,128)S(1)}, f32[10,8,128]{2,1,0:T(8,128)S(1)}, u32[]{:S(2)}, u32[]{:S(2)}) collective-permute-start(f32[10,8,128]{2,1,0:T(8,128)S(1)} %get-tuple-element.17), channel_id=1, source_target_pairs={{0,0},{32,64},{64,32},{96,96},{1,1},{33,65},{65,33},{97,97},{2,2},... | collective-permute-start | bytes 122888 | tf_op jit(solution)/shard_map/ppermute | solution.py:456

commit v5 on v4

--- a/solution.py
+++ b/solution.py
@@ -168,51 +168,50 @@
 
 def gather_kernel(place_ref, x_ref, fields_ref, top_ref, bottom_ref, across_ref, beside_ref,
                   by_rank_ref, bounds_ref, limits_ref, items_ref, vals_ref, acc_ref, sem):
+    def by_rank(p, g, f):
+        first = (2 * p + g) * 32
+        return x_ref[first:first + 32, f].reshape(128, 128).T
+
+    def keep(p, g, f, value):
+        by_rank_ref[p, f, :, g * 128:g * 128 + 128] = value
+
     for p in range(PAIRS):
         least, most = [], []
         for g in range(2):
-            lanes = slice(g * 128, g * 128 + 128)
-            first = (2 * p + g) * 32
-            fields = [x_ref[first:first + 32, f].reshape(128, 128).T for f in range(5)]
-            live = fields[3] > 0.0
-            fields = [jnp.where(live, v, 0.0) for v in fields]
-            for f, v in enumerate(fields):
-                by_rank_ref[p, f, :, lanes] = v
-            i = row_of(fields[0])
+            mass = by_rank(p, g, 3)
+            live = mass > 0.0
+            cell = jnp.where(live, by_rank(p, g, 0), 0.0)
+            keep(p, g, 3, jnp.where(live, mass, 0.0))
+            keep(p, g, 0, cell)
+            i = row_of(cell)
             least.append(jnp.where(live, i, 1000.0))
             most.append(jnp.where(live, i, -1.0))
         low = jnp.min(jnp.minimum(least[0], least[1]).T, axis=0, keepdims=True)
         high = jnp.max(jnp.maximum(most[0], most[1]).T, axis=0, keepdims=True)
-        bounds_ref[16 * p:16 * p + 8, :] = jnp.broadcast_to(low, (8, 128)).astype(jnp.int32)
-        bounds_ref[16 * p + 8:16 * p + 16, :] = jnp.broadcast_to(high, (8, 128)).astype(jnp.int32)
+        base = jnp.floor(low * 0.125) * 8.0
+        span = shifted(high, -(UNITS - 1), 1) - base
+        starts = (lax.broadcasted_iota(jnp.int32, (1, 128), 1) & (UNITS - 1)) == 0
+        widest = jnp.max(jnp.where(starts, span, -1.0), axis=1, keepdims=True)
+        for n, v in enumerate([base, span, jnp.broadcast_to(widest, (1, 128))]):
+            at = 8 * (3 * p + n)
+            bounds_ref[at:at + 8, :] = jnp.broadcast_to(v, (8, 128)).astype(jnp.int32)
     copy = pltpu.make_async_copy(bounds_ref, limits_ref, sem)
     copy.start()
     acc_ref[...] = jnp.zeros_like(acc_ref)
+    for p in range(PAIRS):
+        for g in range(2):
+            live = by_rank_ref[p, 3, :, g * 128:g * 128 + 128] > 0.0
+            for f in (1, 2, 4):
+                keep(p, g, f, jnp.where(live, by_rank(p, g, f), 0.0))
     copy.wait()
 
-    count = jnp.int32(0)
-    for q in range(STEPS):
-        for p in range(PAIRS):
-            first = limits_ref[16 * p, q * UNITS]
-            last = limits_ref[16 * p + 8, q * UNITS + UNITS - 1]
-            base = (first // 8) * 8
-            for w in range(WINDOWS):
-                items_ref[0, count] = q * UNITS
-                items_ref[1, count] = base + w * WINDOW
-                items_ref[2, count] = p
-                count = count + (base + w * WINDOW <= last).astype(jnp.int32)
-    items_ref[0, count] = 0
-    items_ref[1, count] = 1000
-    items_ref[2, count] = 0
-
     sub = lax.broadcasted_iota(jnp.int32, (8, 128), 0)
 
-    def item(t, half):
-        rank = pl.multiple_of(items_ref[0, t], UNITS)
-        base = items_ref[1, t]
+    def item(rank, pair, base, half):
+        rank = pl.multiple_of(rank, UNITS)
         lefts, rights = [], []
         for g in range(2):
-            more = build(rank, base, items_ref[2, t], g, by_rank_ref, vals_ref.at[half])
+            more = build(rank, base, pair, g, by_rank_ref, vals_ref.at[half])
             lefts += more[0]
             rights += more[1]
         out = lax.dot_general(
@@ -233,18 +232,39 @@
                 rows = pl.ds(k * REACH + base + (h + 1) * HALF, 8)
                 acc_ref[rows, :] += jnp.where(sub == 0, out[SPILL + k:SPILL + k + 1, h * 128:(h + 1) * 128], 0.0)
 
-    def four(c, _):
+    def eight(c, _):
         for n in range(8):
-            item(8 * c + n, n)
+            rank = (4 * c + n // 2) * UNITS
+            item(rank, n % 2, limits_ref[24 * (n % 2), rank], n)
         return 0
 
-    def two(c, _):
-        for n in range(2):
-            item(2 * c + n, n)
-        return 0
-
-    lax.fori_loop(0, count // 8, four, 0)
-    lax.fori_loop(4 * (count // 8), (count + 1) // 2, two, 0)
+    lax.fori_loop(0, PAIRS * STEPS // 8, eight, 0)
+
+    @pl.when((limits_ref[16, 0] >= WINDOW) | (limits_ref[40, 0] >= WINDOW))
+    def _():
+        def listed(q, count):
+            for p in range(PAIRS):
+                base = limits_ref[24 * p, q * UNITS]
+                span = limits_ref[24 * p + 8, q * UNITS]
+                for w in range(1, WINDOWS):
+                    items_ref[0, count] = q * UNITS
+                    items_ref[1, count] = base + w * WINDOW
+                    items_ref[2, count] = p
+                    count = count + (span >= w * WINDOW).astype(jnp.int32)
+            return count
+
+        count = lax.fori_loop(0, STEPS, listed, jnp.int32(0))
+        items_ref[0, count] = 0
+        items_ref[1, count] = 1000
+        items_ref[2, count] = 0
+
+        def two(c, _):
+            for n in range(2):
+                t = 2 * c + n
+                item(items_ref[0, t], items_ref[2, t], items_ref[1, t], n)
+            return 0
+
+        lax.fori_loop(0, (count + 1) // 2, two, 0)
 
     def band(k):
         return acc_ref[k * REACH:k * REACH + TR, :]
@@ -347,8 +367,8 @@
     for k in range(4):
         basis_ref[k] = own[k]
     pairs = [(0, 0), (0, 1), (1, 1), (1, 2), (2, 2), (2, 3)]
-    lane = lax.broadcasted_iota(jnp.int32, (TILES, 128), 1)
-    out = jnp.zeros((TILES, 128), f32)
+    lane = lax.broadcasted_iota(jnp.int32, (TILES, 8), 1)
+    out = jnp.zeros((TILES, 8), f32)
     for k, (p, q) in enumerate(pairs):
         m = jnp.sum(jnp.sum(own[p] * own[q], axis=0, keepdims=True), axis=1, keepdims=True)
         out = jnp.where(lane == k, m, out)
@@ -432,8 +452,8 @@
         out_specs=[whole()] * 5,
         scratch_shapes=[
             pltpu.VMEM((PAIRS, 5, 128, 256), f32),
-            pltpu.VMEM((16 * PAIRS, 128), jnp.int32),
-            pltpu.SMEM((16 * PAIRS, 128), jnp.int32),
+            pltpu.VMEM((24 * PAIRS, 128), jnp.int32),
+            pltpu.SMEM((24 * PAIRS, 128), jnp.int32),
             pltpu.SMEM((3, PAIRS * STEPS * WINDOWS + 8), jnp.int32),
             pltpu.VMEM((8, 2, 28 * UNITS, 128), f32),
             pltpu.VMEM((BANDS * REACH, 128), f32),
@@ -457,7 +477,7 @@
     across_n = lax.ppermute(to_across, "north", north_across)
     basis, moments = pl.pallas_call(
         krylov_kernel,
-        out_shape=[jax.ShapeDtypeStruct((4, TR, TC), f32), jax.ShapeDtypeStruct((TILES, 128), f32)],
+        out_shape=[jax.ShapeDtypeStruct((4, TR, TC), f32), jax.ShapeDtypeStruct((TILES, 8), f32)],
         in_specs=[whole()] * 6,
         out_specs=[whole()] * 2,
         compiler_params=params,

time: 88.5 us -> 88.7 us (level)
  blocking collectives: 17 us -> 19.1 us
    all_to_all x1, blocking collectives: 17 us -> 19.1 us  [body(): lax.all_to_all(moments, AXES, split_axis=0, concat_axis=0, tiled=True)]
    ppermute x1, starting transfers between devices: 2.53 us -> 1.41 us  [body(): across_e = lax.ppermute(across, 'east', east_across)]
where the time goes in v5:
time: 88.7 us; the launch traced here: 88.2 us
  waiting for transfers between devices  26.5 us (30%)
  Pallas kernels  25.1 us (28%)
  blocking collectives  19.1 us (22%)
  starting transfers between devices  16 us (18%)
  between operations  1.34 us (2%)
    all_to_all x1, waiting for transfers between devices, body(): got = lax.all_to_all(send, AXES, split_axis=0, concat_axis=0, tiled=True)  21.7 us
    all_to_all x1, blocking collectives, body(): lax.all_to_all(moments, AXES, split_axis=0, concat_axis=0, tiled=True)  19.1 us
    pallas_call x1, Pallas kernels, body(): pl.pallas_call(gather_kernel, out_shape=[jax.ShapeDtypeStruct((5, TR, TC)...  17.6 us
    all_to_all x1, starting transfers between devices, body(): got = lax.all_to_all(send, AXES, split_axis=0, concat_axis=0, tiled=True)  11.5 us
    pallas_call x1, Pallas kernels, body(): pl.pallas_call(route_kernel, out_shape=pltpu.VMEM((TILES, 5, MOST, 128),...  4.87 us
    ppermute x1, waiting for transfers between devices, body(): beside_e = lax.ppermute(beside, 'east', east_beside)  3.15 us
    ppermute x1, starting transfers between devices, body(): beside_e = lax.ppermute(beside, 'east', east_beside)  1.93 us
  transfers between devices with their start and end apart: 5, of which 3 were waited for; matrix products, arithmetic and copies ran while one was open for 0% of the time, Pallas kernels for 0%

profile of v5, /device:TPU:1, one launch (start us, length us, event | category | flops | bytes accessed | tf_op | source)
XLA Modules:
  0.0 88.2 jit_solution(15829826667776589864)
XLA Ops:
  1.3 4.9 %shard_map.77 = f32[128,5,4,128]{3,2,1,0:T(4,128)} custom-call(s32[256]{0:T(256)} %bitcast.7, s32[1]{0:T(128)S(6)} %copy.9.count_ref, s32[256,128]{1,0:T(8,128)} %cells_hbm.1, f32[256,2,128]{2,1,0:T(2,128)} %frac_hbm.1, f32[256,128]{1,0:T(8,128)} %weight_hbm.1, f32[256,128]{1,0:T(8,128)} %height_hbm.1), custom_call_target="tpu_custom_call" | custom-call | tf_op jit(solution)/shard_map/pallas_call | solution.py:428
  6.2 11.5 %all-to-all-start = ((f32[128,5,4,128]{3,2,1,0:T(4,128)}), f32[128,5,4,128]{3,2,1,0:T(4,128)S(1)}, u32[]{:S(2)}, u32[]{:S(2)}) async-start(f32[128,5,4,128]{3,2,1,0:T(4,128)} %shard_map.77), calls=%async_computation | async-start | bytes 2621440 | tf_op jit(solution)/shard_map/all_to_all | solution.py:446
  17.7 21.7 %all-to-all-done.x_ref = f32[128,5,4,128]{3,2,1,0:T(4,128)S(1)} async-done(((f32[128,5,4,128]{3,2,1,0:T(4,128)}), f32[128,5,4,128]{3,2,1,0:T(4,128)S(1)}, u32[]{:S(2)}, u32[]{:S(2)}) %all-to-all-start) | async-done | bytes 1310752 | tf_op jit(solution)/shard_map/all_to_all | solution.py:446
  39.3 0.1 iota.7.place_ref
  39.4 17.6 %shard_map.78 = (f32[5,128,128]{2,1,0:T(8,128)S(1)}, f32[5,8,128]{2,1,0:T(8,128)S(1)}, f32[5,8,128]{2,1,0:T(8,128)S(1)}, f32[5,8,128]{2,1,0:T(8,128)S(1)}, f32[5,8,128]{2,1,0:T(8,128)S(1)}) custom-call(s32[16,128]{1,0:T(8,128)S(1)} %iota.7.place_ref, f32[128,5,4,128]{3,2,1,0:T(4,128)S(1)} %all-to-all-done.x_ref), custom_call_target="tpu_custom_call" | custom-call | tf_op jit(solution)/shard_map/pallas_call | solution.py:448
  57.0 1.4 %collective-permute-start = (f32[5,8,128]{2,1,0:T(8,128)S(1)}, f32[5,8,128]{2,1,0:T(8,128)S(1)}, u32[]{:S(2)}, u32[]{:S(2)}) collective-permute-start(f32[5,8,128]{2,1,0:T(8,128)S(1)} %get-tuple-element.12), channel_id=1, source_target_pairs={{0,1},{1,0},{2,3},{3,2},{4,5},{5,4},{6,7},{7,6},{8,9},{9,8},{10,11... | collective-permute-start | bytes 61448 | tf_op jit(solution)/shard_map/ppermute | solution.py:467
  58.4 1.9 %collective-permute-start.1 = (f32[5,8,128]{2,1,0:T(8,128)S(1)}, f32[5,8,128]{2,1,0:T(8,128)S(1)}, u32[]{:S(2)}, u32[]{:S(2)}) collective-permute-start(f32[5,8,128]{2,1,0:T(8,128)S(1)} %get-tuple-element.13), channel_id=1, source_target_pairs={{0,0},{1,2},{2,1},{3,4},{4,3},{5,6},{6,5},{7,8},{8,7},{9,10},{10,9... | collective-permute-start | bytes 61448 | tf_op jit(solution)/shard_map/ppermute | solution.py:466
  60.4 0.0 collective-permute-done.across_ref.across_e_ref
  60.4 3.1 %collective-permute-done.1.beside_ref.beside_e_ref = f32[5,8,128]{2,1,0:T(8,128)S(1)} collective-permute-done((f32[5,8,128]{2,1,0:T(8,128)S(1)}, f32[5,8,128]{2,1,0:T(8,128)S(1)}, u32[]{:S(2)}, u32[]{:S(2)}) %collective-permute-start.1) | collective-permute-done | bytes 20512 | tf_op jit(solution)/shard_map/ppermute | solution.py:466
  63.5 0.1 shard_map.79
  63.6 0.5 collective-permute-start.2
  64.1 0.7 collective-permute-start.3
  64.8 1.7 %collective-permute-done.2.across_n_ref = f32[10,8,128]{2,1,0:T(8,128)S(1)} collective-permute-done((f32[10,8,128]{2,1,0:T(8,128)S(1)}, f32[10,8,128]{2,1,0:T(8,128)S(1)}, u32[]{:S(2)}, u32[]{:S(2)}) %collective-permute-start.2) | collective-permute-done | bytes 40992 | tf_op jit(solution)/shard_map/ppermute | solution.py:477
  66.5 0.0 collective-permute-done.3.beside_n_ref
  66.5 1.7 %shard_map.80 = (f32[4,128,128]{2,1,0:T(8,128)S(1)}, f32[128,8]{1,0:T(8,128)S(1)}) custom-call(s32[16,128]{1,0:T(8,128)S(1)} %iota.7.place_ref, f32[5,128,128]{2,1,0:T(8,128)S(1)} %get-tuple-element.11.fields_ref, f32[5,8,128]{2,1,0:T(8,128)S(1)} %collective-permute-done.across_ref.across_e_ref, ...), custom_call_target="tpu_custom_call" | custom-call | tf_op jit(solution)/shard_map/pallas_call | solution.py:478
  68.2 19.1 %all_to_all.16 = f32[128,1,8]{2,1,0:T(1,128)S(1)} all-to-all(f32[128,1,8]{2,1,0:T(1,128)S(1)} %bitcast.6), channel_id=1, replica_groups=mesh['north'=4,'east'=32] {'north','east'}, dimensions={0} | all-to-all | bytes 8192 | tf_op jit(solution)/shard_map/all_to_all | solution.py:485
  87.3 0.9 shard_map.81
  (1 shorter events, 0.0 us)
Async XLA Ops:
  6.2 33.2 %all-to-all-start = ((f32[128,5,4,128]{3,2,1,0:T(4,128)}), f32[128,5,4,128]{3,2,1,0:T(4,128)S(1)}, u32[]{:S(2)}, u32[]{:S(2)}) async-start(f32[128,5,4,128]{3,2,1,0:T(4,128)} %shard_map.77), calls=%async_computation | async-start | bytes 2621440 | tf_op jit(solution)/shard_map/all_to_all | solution.py:446
  57.0 3.3 %collective-permute-start = (f32[5,8,128]{2,1,0:T(8,128)S(1)}, f32[5,8,128]{2,1,0:T(8,128)S(1)}, u32[]{:S(2)}, u32[]{:S(2)}) collective-permute-start(f32[5,8,128]{2,1,0:T(8,128)S(1)} %get-tuple-element.12), channel_id=1, source_target_pairs={{0,1},{1,0},{2,3},{3,2},{4,5},{5,4},{6,7},{7,6},{8,9},{9,8},{10,11... | collective-permute-start | bytes 61448 | tf_op jit(solution)/shard_map/ppermute | solution.py:467
  58.4 5.1 %collective-permute-start.1 = (f32[5,8,128]{2,1,0:T(8,128)S(1)}, f32[5,8,128]{2,1,0:T(8,128)S(1)}, u32[]{:S(2)}, u32[]{:S(2)}) collective-permute-start(f32[5,8,128]{2,1,0:T(8,128)S(1)} %get-tuple-element.13), channel_id=1, source_target_pairs={{0,0},{1,2},{2,1},{3,4},{4,3},{5,6},{6,5},{7,8},{8,7},{9,10},{10,9... | collective-permute-start | bytes 61448 | tf_op jit(solution)/shard_map/ppermute | solution.py:466
  63.6 2.9 %collective-permute-start.2 = (f32[10,8,128]{2,1,0:T(8,128)S(1)}, f32[10,8,128]{2,1,0:T(8,128)S(1)}, u32[]{:S(2)}, u32[]{:S(2)}) collective-permute-start(f32[10,8,128]{2,1,0:T(8,128)S(1)} %get-tuple-element.16), channel_id=1, source_target_pairs={{0,32},{32,0},{64,96},{96,64},{1,33},{33,1},{65,97},{97,65},{2,34}... | collective-permute-start | bytes 122888 | tf_op jit(solution)/shard_map/ppermute | solution.py:477
  64.1 2.4 %collective-permute-start.3 = (f32[10,8,128]{2,1,0:T(8,128)S(1)}, f32[10,8,128]{2,1,0:T(8,128)S(1)}, u32[]{:S(2)}, u32[]{:S(2)}) collective-permute-start(f32[10,8,128]{2,1,0:T(8,128)S(1)} %get-tuple-element.17), channel_id=1, source_target_pairs={{0,0},{32,64},{64,32},{96,96},{1,1},{33,65},{65,33},{97,97},{2,2},... | collective-permute-start | bytes 122888 | tf_op jit(solution)/shard_map/ppermute | solution.py:476

commit v6 on v5

--- a/solution.py
+++ b/solution.py
@@ -353,12 +353,13 @@
         u_d = shifted(u, -1, 0)
         u_u = shifted(u, 1, 0)
         lu = laplace(u, u_l, u_r, u_u, u_d)
-        llu = laplace(lu, shifted(lu, 1, 1), shifted(lu, -1, 1), shifted(lu, 1, 0), shifted(lu, -1, 0))
+        near = shifted(lu, 1, 1) + shifted(lu, -1, 1) + shifted(lu, 1, 0) + shifted(lu, -1, 0)
+        smooth = jnp.where(inside, (1.0 - TENSION) * near - (4.0 * (1.0 - TENSION) + TENSION) * lu, 0.0)
         u_rd = shifted(u_r, -1, 0)
         out = diag * u + along_east * u_r + along_south * u_d + cross * u_rd
         out = out + shifted(along_east * u + cross * u_d, 1, 1)
         out = out + shifted(along_south * u + cross * u_r + shifted(cross * u, 1, 1), 1, 0)
-        return (out + (1.0 - TENSION) * llu - TENSION * lu) * SHRINK
+        return (out + smooth) * SHRINK
 
     v = [v0]
     for _ in range(3):
@@ -378,38 +379,23 @@
 def finish_kernel(moments_ref, basis_ref, surface_ref, residual_ref):
     total = jnp.sum(moments_ref[...], axis=0, keepdims=True)
     m = [total[:, k:k + 1] for k in range(6)]
-
-    def dot(p, q, shift):
-        terms = [p[a] * q[b] * m[a + b + shift] for a in range(len(p)) for b in range(len(q))]
-        s = terms[0]
-        for t in terms[1:]:
-            s = s + t
-        return s
-
-    one = jnp.ones_like(m[0])
-    res = [one]
-    direction = [one]
-    surf = []
-    rr = m[0]
-    for it in range(3):
-        alpha = rr / dot(direction, direction, 1)
-        surf = [(surf[k] if k < len(surf) else 0.0) + alpha * direction[k] for k in range(len(direction))]
-        stepped = [jnp.zeros_like(one)] + [alpha * c for c in direction]
-        res = [(res[k] if k < len(res) else 0.0) - stepped[k] for k in range(len(stepped))]
-        if it < 2:
-            fresh = dot(res, res, 0)
-            beta = fresh / rr
-            direction = [res[k] + (beta * direction[k] if k < len(direction) else 0.0) for k in range(len(res))]
-            rr = fresh
+    a0 = m[1] / m[0]
+    sigma1 = {n: m[n + 1] - a0 * m[n] for n in range(1, 5)}
+    ratio1 = sigma1[2] / sigma1[1]
+    b1 = sigma1[1] / m[0]
+    a1 = ratio1 - a0
+    sigma2 = {n: (sigma1[n + 1] - a1 * sigma1[n]) - b1 * m[n] for n in (2, 3)}
+    a2 = sigma2[3] / sigma2[2] - ratio1
+    b2 = sigma2[2] / sigma1[1]
+    both = a0 + a1
+    flat = a0 * a1 - b1
+    c2 = both + a2
+    c1 = (flat + a2 * both) - b2
+    third = 1.0 / (a2 * flat - b2 * a0)
+    first, second = c1 * third, c2 * third
     basis = [basis_ref[k] for k in range(4)]
-    out = (surf[0] * SHRINK) * basis[0]
-    for k in range(1, 3):
-        out = out + (surf[k] * SHRINK) * basis[k]
-    surface_ref[...] = out
-    out = res[0] * basis[0]
-    for k in range(1, 4):
-        out = out + res[k] * basis[k]
-    residual_ref[...] = out
+    surface_ref[...] = SHRINK * ((first * basis[0] - second * basis[1]) + third * basis[2])
+    residual_ref[...] = ((basis[0] - first * basis[1]) + second * basis[2]) - third * basis[3]
 
 
 def swaps(count):

time: 88.7 us -> 89.4 us (level)
  no operation moved by 1% of the time
where the time goes in v6:
time: 89.4 us; the launch traced here: 89.1 us
  waiting for transfers between devices  26.4 us (30%)
  Pallas kernels  25.5 us (29%)
  blocking collectives  19.7 us (22%)
  starting transfers between devices  16.1 us (18%)
  between operations  1.34 us (1%)
    all_to_all x1, waiting for transfers between devices, body(): got = lax.all_to_all(send, AXES, split_axis=0, concat_axis=0, tiled=True)  21.7 us
    all_to_all x1, blocking collectives, body(): lax.all_to_all(moments, AXES, split_axis=0, concat_axis=0, tiled=True)  19.7 us
    pallas_call x1, Pallas kernels, body(): pl.pallas_call(gather_kernel, out_shape=[jax.ShapeDtypeStruct((5, TR, TC)...  17.6 us
    all_to_all x1, starting transfers between devices, body(): got = lax.all_to_all(send, AXES, split_axis=0, concat_axis=0, tiled=True)  11.5 us
    pallas_call x1, Pallas kernels, body(): pl.pallas_call(route_kernel, out_shape=pltpu.VMEM((TILES, 5, MOST, 128),...  4.87 us
    ppermute x1, waiting for transfers between devices, body(): beside_e = lax.ppermute(beside, 'east', east_beside)  3.13 us
    ppermute x1, starting transfers between devices, body(): beside_e = lax.ppermute(beside, 'east', east_beside)  1.94 us
  transfers between devices with their start and end apart: 5, of which 3 were waited for; matrix products, arithmetic and copies ran while one was open for 0% of the time, Pallas kernels for 0%

profile of v6, /device:TPU:1, one launch (start us, length us, event | category | flops | bytes accessed | tf_op | source)
XLA Modules:
  0.0 89.1 jit_solution(15255228269431300983)
XLA Ops:
  1.3 4.9 %shard_map.77 = f32[128,5,4,128]{3,2,1,0:T(4,128)} custom-call(s32[256]{0:T(256)} %bitcast.7, s32[1]{0:T(128)S(6)} %copy.9.count_ref, s32[256,128]{1,0:T(8,128)} %cells_hbm.1, f32[256,2,128]{2,1,0:T(2,128)} %frac_hbm.1, f32[256,128]{1,0:T(8,128)} %weight_hbm.1, f32[256,128]{1,0:T(8,128)} %height_hbm.1), custom_call_target="tpu_custom_call" | custom-call | tf_op jit(solution)/shard_map/pallas_call | solution.py:414
  6.2 11.5 %all-to-all-start = ((f32[128,5,4,128]{3,2,1,0:T(4,128)}), f32[128,5,4,128]{3,2,1,0:T(4,128)S(1)}, u32[]{:S(2)}, u32[]{:S(2)}) async-start(f32[128,5,4,128]{3,2,1,0:T(4,128)} %shard_map.77), calls=%async_computation | async-start | bytes 2621440 | tf_op jit(solution)/shard_map/all_to_all | solution.py:432
  17.7 21.7 %all-to-all-done.x_ref = f32[128,5,4,128]{3,2,1,0:T(4,128)S(1)} async-done(((f32[128,5,4,128]{3,2,1,0:T(4,128)}), f32[128,5,4,128]{3,2,1,0:T(4,128)S(1)}, u32[]{:S(2)}, u32[]{:S(2)}) %all-to-all-start) | async-done | bytes 1310752 | tf_op jit(solution)/shard_map/all_to_all | solution.py:432
  39.3 0.1 iota.7.place_ref
  39.4 17.6 %shard_map.78 = (f32[5,128,128]{2,1,0:T(8,128)S(1)}, f32[5,8,128]{2,1,0:T(8,128)S(1)}, f32[5,8,128]{2,1,0:T(8,128)S(1)}, f32[5,8,128]{2,1,0:T(8,128)S(1)}, f32[5,8,128]{2,1,0:T(8,128)S(1)}) custom-call(s32[16,128]{1,0:T(8,128)S(1)} %iota.7.place_ref, f32[128,5,4,128]{3,2,1,0:T(4,128)S(1)} %all-to-all-done.x_ref), custom_call_target="tpu_custom_call" | custom-call | tf_op jit(solution)/shard_map/pallas_call | solution.py:434
  57.0 1.4 %collective-permute-start = (f32[5,8,128]{2,1,0:T(8,128)S(1)}, f32[5,8,128]{2,1,0:T(8,128)S(1)}, u32[]{:S(2)}, u32[]{:S(2)}) collective-permute-start(f32[5,8,128]{2,1,0:T(8,128)S(1)} %get-tuple-element.12), channel_id=1, source_target_pairs={{0,1},{1,0},{2,3},{3,2},{4,5},{5,4},{6,7},{7,6},{8,9},{9,8},{10,11... | collective-permute-start | bytes 61448 | tf_op jit(solution)/shard_map/ppermute | solution.py:453
  58.4 1.9 %collective-permute-start.1 = (f32[5,8,128]{2,1,0:T(8,128)S(1)}, f32[5,8,128]{2,1,0:T(8,128)S(1)}, u32[]{:S(2)}, u32[]{:S(2)}) collective-permute-start(f32[5,8,128]{2,1,0:T(8,128)S(1)} %get-tuple-element.13), channel_id=1, source_target_pairs={{0,0},{1,2},{2,1},{3,4},{4,3},{5,6},{6,5},{7,8},{8,7},{9,10},{10,9... | collective-permute-start | bytes 61448 | tf_op jit(solution)/shard_map/ppermute | solution.py:452
  60.3 0.0 collective-permute-done.across_ref.across_e_ref
  60.3 3.1 %collective-permute-done.1.beside_ref.beside_e_ref = f32[5,8,128]{2,1,0:T(8,128)S(1)} collective-permute-done((f32[5,8,128]{2,1,0:T(8,128)S(1)}, f32[5,8,128]{2,1,0:T(8,128)S(1)}, u32[]{:S(2)}, u32[]{:S(2)}) %collective-permute-start.1) | collective-permute-done | bytes 20512 | tf_op jit(solution)/shard_map/ppermute | solution.py:452
  63.5 0.1 shard_map.79
  63.6 0.6 collective-permute-start.2
  64.1 0.7 collective-permute-start.3
  64.8 1.6 %collective-permute-done.2.across_n_ref = f32[10,8,128]{2,1,0:T(8,128)S(1)} collective-permute-done((f32[10,8,128]{2,1,0:T(8,128)S(1)}, f32[10,8,128]{2,1,0:T(8,128)S(1)}, u32[]{:S(2)}, u32[]{:S(2)}) %collective-permute-start.2) | collective-permute-done | bytes 40992 | tf_op jit(solution)/shard_map/ppermute | solution.py:463
  66.4 0.0 collective-permute-done.3.beside_n_ref
  66.4 1.7 %shard_map.80 = (f32[4,128,128]{2,1,0:T(8,128)S(1)}, f32[128,8]{1,0:T(8,128)S(1)}) custom-call(s32[16,128]{1,0:T(8,128)S(1)} %iota.7.place_ref, f32[5,128,128]{2,1,0:T(8,128)S(1)} %get-tuple-element.11.fields_ref, f32[5,8,128]{2,1,0:T(8,128)S(1)} %collective-permute-done.across_ref.across_e_ref, ...), custom_call_target="tpu_custom_call" | custom-call | tf_op jit(solution)/shard_map/pallas_call | solution.py:464
  68.2 19.7 %all_to_all.16 = f32[128,1,8]{2,1,0:T(1,128)S(1)} all-to-all(f32[128,1,8]{2,1,0:T(1,128)S(1)} %bitcast.6), channel_id=1, replica_groups=mesh['north'=4,'east'=32] {'north','east'}, dimensions={0} | all-to-all | bytes 8192 | tf_op jit(solution)/shard_map/all_to_all | solution.py:471
  87.8 1.2 %shard_map.81 = (f32[128,128]{1,0:T(8,128)}, f32[128,128]{1,0:T(8,128)}) custom-call(f32[128,8]{1,0:T(8,128)S(1)} %bitcast.5, f32[4,128,128]{2,1,0:T(8,128)S(1)} %get-tuple-element.19.basis_ref), custom_call_target="tpu_custom_call" | custom-call | tf_op jit(solution)/shard_map/pallas_call | solution.py:472
  (1 shorter events, 0.0 us)
Async XLA Ops:
  6.2 33.2 %all-to-all-start = ((f32[128,5,4,128]{3,2,1,0:T(4,128)}), f32[128,5,4,128]{3,2,1,0:T(4,128)S(1)}, u32[]{:S(2)}, u32[]{:S(2)}) async-start(f32[128,5,4,128]{3,2,1,0:T(4,128)} %shard_map.77), calls=%async_computation | async-start | bytes 2621440 | tf_op jit(solution)/shard_map/all_to_all | solution.py:432
  57.0 3.3 %collective-permute-start = (f32[5,8,128]{2,1,0:T(8,128)S(1)}, f32[5,8,128]{2,1,0:T(8,128)S(1)}, u32[]{:S(2)}, u32[]{:S(2)}) collective-permute-start(f32[5,8,128]{2,1,0:T(8,128)S(1)} %get-tuple-element.12), channel_id=1, source_target_pairs={{0,1},{1,0},{2,3},{3,2},{4,5},{5,4},{6,7},{7,6},{8,9},{9,8},{10,11... | collective-permute-start | bytes 61448 | tf_op jit(solution)/shard_map/ppermute | solution.py:453
  58.4 5.1 %collective-permute-start.1 = (f32[5,8,128]{2,1,0:T(8,128)S(1)}, f32[5,8,128]{2,1,0:T(8,128)S(1)}, u32[]{:S(2)}, u32[]{:S(2)}) collective-permute-start(f32[5,8,128]{2,1,0:T(8,128)S(1)} %get-tuple-element.13), channel_id=1, source_target_pairs={{0,0},{1,2},{2,1},{3,4},{4,3},{5,6},{6,5},{7,8},{8,7},{9,10},{10,9... | collective-permute-start | bytes 61448 | tf_op jit(solution)/shard_map/ppermute | solution.py:452
  63.6 2.9 %collective-permute-start.2 = (f32[10,8,128]{2,1,0:T(8,128)S(1)}, f32[10,8,128]{2,1,0:T(8,128)S(1)}, u32[]{:S(2)}, u32[]{:S(2)}) collective-permute-start(f32[10,8,128]{2,1,0:T(8,128)S(1)} %get-tuple-element.16), channel_id=1, source_target_pairs={{0,32},{32,0},{64,96},{96,64},{1,33},{33,1},{65,97},{97,65},{2,34}... | collective-permute-start | bytes 122888 | tf_op jit(solution)/shard_map/ppermute | solution.py:463
  64.1 2.3 %collective-permute-start.3 = (f32[10,8,128]{2,1,0:T(8,128)S(1)}, f32[10,8,128]{2,1,0:T(8,128)S(1)}, u32[]{:S(2)}, u32[]{:S(2)}) collective-permute-start(f32[10,8,128]{2,1,0:T(8,128)S(1)} %get-tuple-element.17), channel_id=1, source_target_pairs={{0,0},{32,64},{64,32},{96,96},{1,1},{33,65},{65,33},{97,97},{2,2},... | collective-permute-start | bytes 122888 | tf_op jit(solution)/shard_map/ppermute | solution.py:462
